TPU v7x, 256 devices: a whole 4x4x8 slice. The times are simulated.
256 devices in a mesh: dp: 8 (over y, x_hi), seq: 32 (over z, x_lo, core).
Axes of the slice: x: 4 (x_hi: 2, x_lo: 2; x = x_hi * 2 + x_lo), y: 4, z: 8, core: 2. Of those that a mesh axis runs over, the one named last changes fastest.
Arguments:
- hidden: bfloat16 [1024, 4096], P('dp')
- gain: float32 [4096], replicated, may hold values from 0.5 to 1.5
- head_weight: bfloat16 [84224, 4096], P('seq', 'dp')
- targets: int32 [1024], P('dp'), may hold values from 0 to 84223
- loss_mask: int32 [1024], P('dp'), may hold values from 0 to 1, as said below
Outputs:
- loss: float32 [], replicated
- grad_hidden: bfloat16 [1024, 4096], P('dp')
- grad_gain: float32 [4096], replicated
- grad_head: float32 [84224, 4096], P('seq', 'dp')
Inputs may be any that keep to these rules, and one draw needn't show every extreme that they name: `loss_mask`: position 0 is valid; the share of valid positions rises from about a quarter at the first position to about three quarters at the last.
All inputs are finite; a program needn't handle non-finite values.
Results may differ from a plain program's by a relative error of at most 0.0049.
Values may be sent and summed in bfloat16 or wider, within the bound.
A program may use at most 64 MiB of HBM per device.

v0:
```python
import jax
import jax.numpy as jnp
from jax import lax
from jax.sharding import PartitionSpec as P

EPS = 1e-05


def norm_back(grad_normed, unit_rows, inv_rms, gain):
    grad_unit = grad_normed * gain
    return inv_rms * (
        grad_unit - unit_rows * jnp.mean(grad_unit * unit_rows, axis=-1, keepdims=True)
    )


def body(hidden, gain, head_weight, targets, loss_mask):
    floats = hidden.astype(jnp.float32)
    inv_rms = lax.rsqrt(jnp.mean(floats * floats, axis=-1, keepdims=True) + EPS)
    unit_rows = floats * inv_rms
    normed = (unit_rows * gain).astype(jnp.bfloat16)
    mask_float = loss_mask.astype(jnp.float32)
    num_valid = lax.psum(jnp.sum(mask_float), "dp")
    slices = lax.all_to_all(normed, "dp", split_axis=1, concat_axis=0, tiled=True)
    vocab_rows = head_weight.shape[0]
    chosen = slices
    logits = lax.psum_scatter(
        lax.dot_general(
            chosen, head_weight, (((1,), (1,)), ((), ())), preferred_element_type=jnp.float32
        ),
        "dp",
        scatter_dimension=0,
        tiled=True,
    )
    column = lax.axis_index("seq") * vocab_rows + jnp.arange(vocab_rows, dtype=jnp.int32)
    one_hot = (column[None, :] == targets[:, None]).astype(jnp.float32)
    local_picked = jnp.sum(one_hot * logits, axis=1)
    local_top = jnp.max(logits, axis=1)
    row_top = lax.pmax(local_top, "seq")
    shifted = jnp.exp(logits - row_top[:, None])
    row_total, picked = lax.psum((jnp.sum(shifted, axis=1), local_picked), "seq")
    log_total = row_top + jnp.log(row_total)
    probs = shifted / row_total[:, None]
    row_loss = log_total - picked
    loss_value = lax.psum(jnp.sum(mask_float * row_loss), "dp") / num_valid
    dlogits = ((probs - one_hot) * (mask_float / num_valid)[:, None]).astype(jnp.bfloat16)
    shard_rows = lax.all_gather(dlogits, "dp", axis=0, tiled=True)
    chosen = slices
    row_part = jnp.dot(shard_rows, head_weight, preferred_element_type=jnp.float32)
    grad_slices = row_part
    grad_weight = lax.dot_general(
        shard_rows, chosen, (((0,), (0,)), ((), ())), preferred_element_type=jnp.float32
    )
    grad_slices, grad_head = (grad_slices, grad_weight)
    returned = lax.all_to_all(grad_slices, "dp", split_axis=0, concat_axis=1, tiled=True)
    grad_normed = lax.psum(returned, "seq")
    grad_gain = lax.psum(jnp.sum(grad_normed * unit_rows, axis=0), "dp")
    grad_hidden = norm_back(grad_normed, unit_rows, inv_rms, gain).astype(jnp.bfloat16)
    return (loss_value, grad_hidden, grad_gain, grad_head)


def solution(mesh):
    return jax.shard_map(
        body,
        mesh=mesh,
        in_specs=(P("dp", None), P(), P("seq", "dp"), P("dp"), P("dp")),
        out_specs=(P(), P("dp", None), P(), P("seq", "dp")),
        check_vma=False,
    )
```

profile of v0, /device:TPU:0, one launch (start us, length us, event | category | flops | bytes accessed | tf_op | source)
XLA Modules:
  0.0 739.4 jit_solution(16655431562277468732)
XLA Ops:
  7.2 0.0 copy-start
  7.2 0.0 copy-start.3
  7.2 0.0 reduce-scatter.2.cloned.1.call-start
  7.2 2.4 copy.11
  9.7 1.8 fusion.10
  11.4 0.0 copy-done.3
  11.4 1.7 fusion.4
  13.2 22.3 %all_to_all.38 = bf16[128,8,512]{0,2,1:T(8,128)(2,1)} all-to-all(bf16[128,8,512]{0,2,1:T(8,128)(2,1)S(1)} %bitcast.14), channel_id=1, replica_groups=mesh['dp'=8,'seq'=32] {'dp'}, dimensions={1} | all-to-all | bytes 2097152 | tf_op jit(solution)/shard_map/all_to_all | solution.py:23
  35.5 2.3 copy.12
  37.8 0.0 copy-done
  37.8 6.9 fusion.16
  44.7 0.0 copy-start.4
  44.7 0.0 reduce-scatter.2.cloned.1.call-update
  44.7 0.0 copy-start.5
  44.7 0.0 all-gather.2.cloned.1.call-start
  44.8 145.6 %reduce-scatter.2.cloned.1.call-done = f32[128,2632]{0,1:T(8,128)} async-done(((f32[1024,2632]{0,1:T(8,128)}), f32[128,2632]{0,1:T(8,128)}) %reduce-scatter.2.cloned.1.call-update) | async-done | bytes 1347600 | tf_op jit(solution)/shard_map/reduce_scatter | solution.py:26
  190.4 1.7 reduce_max.9
  192.1 55.2 %pmax.7 = f32[128]{0:T(128)S(1)} all-reduce(f32[128]{0:T(128)S(1)} %reduce_max.9), channel_id=1, replica_groups=mesh['dp'=8,'seq'=32] {'seq'}, use_global_device_ids=true, to_apply=%region_3.0 | all-reduce | flops 128 | bytes 1024 | tf_op jit(solution)/shard_map/pmax | solution.py:38
  247.3 0.0 copy-done.4
  247.3 2.3 fusion.15
  249.6 53.0 %all-reduce = (f32[128]{0:T(128)S(1)}, f32[128]{0:T(128)S(1)}) all-reduce(f32[128]{0:T(128)S(1)} %get-tuple-element.11, f32[128]{0:T(128)S(1)} %get-tuple-element.10), channel_id=1, replica_groups=mesh['dp'=8,'seq'=32] {'seq'}, use_global_device_ids=true, to_apply=%region_7.0 | all-reduce | flops 256 | bytes 2048 | tf_op jit(solution)/shard_map/psum | solution.py:40
  302.6 0.0 copy-done.5
  302.6 0.7 convert_reduce_fusion
  303.2 22.0 %psum.45 = f32[]{:T(128)} all-reduce(f32[]{:T(128)} %get-tuple-element.12), channel_id=1, replica_groups=mesh['dp'=8,'seq'=32] {'dp'}, use_global_device_ids=true, to_apply=%region_11.0 | all-reduce | flops 1 | bytes 8 | tf_op jit(solution)/shard_map/psum | solution.py:22
  325.2 0.6 convert_divide_fusion
  325.9 3.0 fusion.14
  328.9 0.0 all-gather.2.cloned.1.call-update
  328.9 0.0 all-reduce.4.cloned.1.call-start
  329.0 85.0 %all-gather.2.cloned.1.call-done = bf16[1024,2632]{0,1:T(8,128)(2,1)} async-done(((bf16[128,2632]{0,1:T(8,128)(2,1)}), bf16[1024,2632]{0,1:T(8,128)(2,1)}) %all-gather.2.cloned.1.call-update) | async-done | bytes 5390352 | tf_op jit(solution)/shard_map/all_gather | solution.py:46
  413.9 5.1 fusion.17
  419.1 31.5 %all_to_all.39 = f32[8,128,512]{2,1,0:T(8,128)} all-to-all(f32[8,128,512]{2,1,0:T(8,128)S(1)} %bitcast.16), channel_id=1, replica_groups=mesh['dp'=8,'seq'=32] {'dp'}, dimensions={0} | all-to-all | bytes 4194304 | tf_op jit(solution)/shard_map/all_to_all | solution.py:54
  450.6 2.9 copy.13
  453.5 0.0 all-reduce.4.cloned.1.call-update
  453.5 8.2 %fusion.18 = f32[2632,512]{1,0:T(8,128)} fusion(bf16[1024,2632]{0,1:T(8,128)(2,1)} %all-gather.2.cloned.1.call-done, bf16[1024,512]{1,0:T(8,128)(2,1)} %bitcast.18), kind=kOutput, calls=%fused_computation.29 | convolution fusion | flops 2759852032 | bytes 11829248 | tf_op jit(solution)/shard_map/dot_general | solution.py:50
  461.7 219.0 %all-reduce.4.cloned.1.call-done = f32[128,4096]{0,1:T(8,128)} async-done(((f32[128,4096]{0,1:T(8,128)}), f32[128,4096]{0,1:T(8,128)}) %all-reduce.4.cloned.1.call-update) | async-done | bytes 2097168 | tf_op jit(solution)/shard_map/psum | solution.py:55
  680.7 0.0 copy-start.1
  680.7 0.0 copy-start.2
  680.7 2.9 fusion.9
  683.6 0.0 copy-done.1
  683.7 0.0 copy-done.2
  683.7 1.5 fusion.8
  685.2 2.3 copy.14
  687.5 43.0 %all-reduce.1 = (f32[]{:T(128)}, f32[4096]{0:T(1024)}) all-reduce(f32[]{:T(128)} %get-tuple-element.13, f32[4096]{0:T(1024)S(1)} %get-tuple-element.8), channel_id=1, replica_groups=mesh['dp'=8,'seq'=32] {'dp'}, use_global_device_ids=true, to_apply=%region_9.0 | all-reduce | flops 4097 | bytes 32776 | tf_op jit(solution)/shard_map/psum | solution.py:44
  (3 shorter events, 0.0 us)
Async XLA Ops:
  7.2 30.6 %copy-start = (bf16[2632,512]{1,0:T(8,128)(2,1)S(1)}, bf16[2632,512]{1,0:T(8,128)(2,1)}, u32[]{:S(2)}) copy-start(bf16[2632,512]{1,0:T(8,128)(2,1)} %param.7) | copy-start | bytes 8085508
  7.2 4.3 copy-start.3
  7.2 183.2 %reduce-scatter.2.cloned.1.call-start = ((), (), s32[]{:S(2)}) async-start(), calls=%async_computation.3 | async-start | bytes 12128256 | tf_op jit(solution)/shard_map/reduce_scatter | solution.py:26
  44.7 202.6 %copy-start.4 = (s32[128]{0:T(128)S(1)}, s32[128]{0:T(128)}, u32[]{:S(2)}) copy-start(s32[128]{0:T(128)} %param.8) | copy-start | bytes 1540
  44.7 257.9 %copy-start.5 = (s32[128]{0:T(128)S(1)}, s32[128]{0:T(128)}, u32[]{:S(2)}) copy-start(s32[128]{0:T(128)} %param.9) | copy-start | bytes 1540
  44.7 369.2 %all-gather.2.cloned.1.call-start = ((), (), s32[]{:S(2)}) async-start(), calls=%async_computation.4 | async-start | bytes 6064128 | tf_op jit(solution)/shard_map/all_gather | solution.py:46
  328.9 351.8 %all-reduce.4.cloned.1.call-start = ((), (), s32[]{:S(2)}) async-start(), calls=%async_computation.5 | async-start | bytes 4194304 | tf_op jit(solution)/shard_map/psum | solution.py:55
  680.7 2.9 copy-start.1
  680.7 3.0 copy-start.2
Sparse Core Ops, SparseCore 0:
  44.8 145.5 reduce-scatter.1
  329.1 84.8 all-gather.1
  453.6 227.0 all-reduce.3
where the time goes:
time: 740 us; the launch traced here: 739 us
  waiting for transfers between devices  450 us (61%)
  blocking collectives  227 us (31%)
  matrix products  20.2 us (3%)
  between operations  16.4 us (2%)
  other arithmetic  16.3 us (2%)
  local copies, waits for them, and re-layouts  9.91 us (1%)
    psum x1, waiting for transfers between devices, body(): grad_normed = lax.psum(returned, 'seq')  219 us
    reduce_scatter x1, waiting for transfers between devices, body(): lax.psum_scatter(lax.dot_general(chosen, head_weight, (((1,), (1,)), ((),...  146 us
    all_gather x1, waiting for transfers between devices, body(): shard_rows = lax.all_gather(dlogits, 'dp', axis=0, tiled=True)  85 us
    pmax x1, blocking collectives, body(): row_top = lax.pmax(local_top, 'seq')  55.2 us
    psum x1, blocking collectives, body(): lax.psum((jnp.sum(shifted, axis=1), local_picked), 'seq')  53 us
    psum x1, blocking collectives, body(): loss_value = lax.psum(jnp.sum(mask_float * row_loss), 'dp') / num_valid  43 us
    all_to_all x1, blocking collectives, body(): lax.all_to_all(grad_slices, 'dp', split_axis=0, concat_axis=1, tiled=True)  31.5 us
    all_to_all x1, blocking collectives, body(): lax.all_to_all(normed, 'dp', split_axis=1, concat_axis=0, tiled=True)  22.3 us
  transfers between devices with their start and end apart: 3, of which 3 were waited for; matrix products, arithmetic and copies ran while one was open for 1% of the time, Pallas kernels for 0%

commit v1 on v0

v1 whole, which is shorter than its diff:
```python
import jax
import jax.numpy as jnp
from jax import lax
from jax.experimental import pallas as pl
from jax.experimental.pallas import tpu as pltpu
from jax.sharding import PartitionSpec as P

EPS = 1e-05
MESH = pl.DeviceIdType.MESH
F32 = jnp.float32
BF16 = jnp.bfloat16
NT = (((1,), (1,)), ((), ()))

D = 4096
W = 512
B = 128
V = 2632
CAP = 640
CH = 7
R = 384
LOW = -1e30

H0, M0, HC0, S10, S20, SX0 = 0, 8, 16, 24, 32, 40
T10, T20, T30, GX0, G20, G10 = 48, 56, 64, 72, 80, 88
DC0, DX0, DZ0, DP0, AZ0, BZ0, AX0, BX0, AC0, BC0 = 96, 97, 104, 112, 120, 128, 136, 137, 138, 139
NSEM = 144


def kernel(hid, gain, wgt, tgt, msk, gh, ghid, gg, scal,
           H, META, WT, S, HC, HCT, C, GCOL, ROWS, L, R1, A1, R2, A2, R3, F, STAT, ST1, ST2, ST3,
           DL, DN, RC, T1, B1, RX, T2, B2, RZ, MB, RB, GT, GG, GH, ss, rs, ls):
    dp = lax.axis_index("dp")
    seq = lax.axis_index("seq")
    y, xh = dp // 2, dp % 2
    z, xl, co = seq // 4, (seq // 2) % 2, seq % 2
    p1, p2 = (y // 2 + y) % 2, y // 2
    ya, yb = y + 1 - 2 * (y % 2), 3 - y
    xpeer = y * 2 + 1 - xh

    def seq_of(zz, xx, cc):
        return zz * 4 + xx * 2 + cc

    def rcopy(src, dst, sem, dev):
        return pltpu.make_async_remote_copy(
            src_ref=src, dst_ref=dst, send_sem=ss.at[sem], recv_sem=rs.at[sem],
            device_id=dev, device_id_type=MESH)

    dp_peers = [lax.rem(dp + k, 8) for k in range(1, 8)]
    dp_from = [lax.rem(dp + 8 - k, 8) for k in range(1, 8)]
    z_peers = [lax.rem(z + k, 8) for k in range(1, 8)]
    z_from = [lax.rem(z + 8 - k, 8) for k in range(1, 8)]
    g_me = xl * 2 + co
    g_peers = [lax.rem(g_me + k, 4) for k in range(1, 4)]
    g_from = [lax.rem(g_me + 4 - k, 4) for k in range(1, 4)]
    core_dev = (dp, seq_of(z, xl, 1 - co))
    xlo_dev = (dp, seq_of(z, 1 - xl, co))

    barrier = pltpu.get_barrier_semaphore()
    for j in dp_peers:
        pl.semaphore_signal(barrier, inc=1, device_id=(j, seq), device_id_type=MESH)
    for g in g_peers:
        pl.semaphore_signal(barrier, inc=1, device_id=(dp, z * 4 + g), device_id_type=MESH)
    for zz in z_peers:
        pl.semaphore_signal(barrier, inc=1, device_id=(dp, seq_of(zz, xl, co)), device_id_type=MESH)
    pl.semaphore_wait(barrier, 17)

    half = pl.ds(pl.multiple_of(co * 64, 64), 64)
    ohalf = pl.ds(pl.multiple_of((1 - co) * 64, 64), 64)
    hsend = []
    for k in range(1, 8):
        j = dp_peers[k - 1]
        c = rcopy(hid.at[half, pl.ds(pl.multiple_of(j * W, W), W)], H.at[dp, half, :], H0 + k, (j, seq))
        c.start()
        hsend.append(c)
    H[dp] = hid[:, pl.ds(pl.multiple_of(dp * W, W), W)]
    total = jnp.zeros((B, 1), F32)
    for j in range(8):
        x = hid[:, j * W:(j + 1) * W].astype(F32)
        total = total + jnp.sum(x * x, axis=1, keepdims=True)
    rinv = lax.rsqrt(total * (1.0 / D) + EPS)
    rinv_t = jnp.transpose(jnp.broadcast_to(rinv, (B, B)))
    META[dp] = jnp.concatenate(
        [rinv_t[0:1, :], msk[...].astype(F32), tgt[...].astype(F32), jnp.zeros((5, B), F32)], axis=0)
    msend = []
    for k in range(1, 8):
        c = rcopy(META.at[dp], META.at[dp], M0 + k, (dp_peers[k - 1], seq))
        c.start()
        msend.append(c)

    @pl.loop(0, CH)
    def _(c):
        rows = pl.ds(pl.multiple_of(c * R, R), R)
        WT[c] = jnp.transpose(wgt[rows, :])
    gain_row = gain[pl.ds(dp, 1), :]
    GCOL[...] = jnp.transpose(jnp.broadcast_to(gain_row, (B, W)))

    hc = []
    for k in range(1, 8):
        j = dp_from[k - 1]
        rcopy(H.at[j, half, :], H.at[j, half, :], H0 + k, (dp, seq)).wait_recv()
        c = rcopy(H.at[j, half, :], H.at[j, half, :], HC0 + k, core_dev)
        c.start()
        hc.append(c)
    for k in range(1, 8):
        j = dp_from[k - 1]
        rcopy(META.at[j], META.at[j], M0 + k, (dp, seq)).wait_recv()

    metas = [META[j] for j in range(8)]
    m8 = jnp.concatenate([m[1:2, :] for m in metas] + [jnp.zeros((8, B), F32)], axis=0)
    tri = (lax.broadcasted_iota(jnp.int32, (B, B), 0) <= lax.broadcasted_iota(jnp.int32, (B, B), 1)).astype(F32)
    cum = jnp.dot(m8.astype(BF16), tri.astype(BF16), preferred_element_type=F32)
    base = jnp.zeros((1, 1), F32)
    slot = lax.broadcasted_iota(jnp.int32, (CAP, B), 0)
    for j in range(8):
        rank = jnp.where(metas[j][1:2, :] > 0.5, cum[j:j + 1, :] + base - 1.0, -1.0).astype(jnp.int32)
        S[:, j * B:(j + 1) * B] = (slot == rank).astype(F32).astype(BF16)
        base = base + jnp.sum(metas[j][1:2, :], axis=1, keepdims=True)
    count = base
    r_all = jnp.concatenate([m[0:1, :] for m in metas], axis=1)
    v_all = jnp.concatenate([m[1:2, :] for m in metas], axis=1)
    t_all = jnp.concatenate([m[2:3, :] for m in metas], axis=1)
    hi = r_all.astype(BF16).astype(F32)
    mid = (r_all - hi).astype(BF16).astype(F32)
    lo = (r_all - hi) - mid
    ta = jnp.floor(t_all * (1.0 / 4096))
    tb = jnp.floor((t_all - ta * 4096) * (1.0 / 64))
    tc = t_all - ta * 4096 - tb * 64
    mr = jnp.concatenate([hi, mid, lo, v_all, ta, tb, tc, jnp.zeros((9, 8 * B), F32)], axis=0).astype(BF16)
    crow = lax.dot_general(mr, S[...], NT, preferred_element_type=F32)
    mr2 = jnp.concatenate([mr, jnp.zeros((B - 16, 8 * B), BF16)], axis=0)
    ccol = lax.dot_general(S[...], mr2, NT, preferred_element_type=F32)
    rinv_row = crow[0:1, :] + crow[1:2, :] + crow[2:3, :]
    valid_row = crow[3:4, :]
    tgt_f = crow[4:5, :] * 4096.0 + crow[5:6, :] * 64.0 + crow[6:7, :]
    tgt_f = jnp.where(valid_row > 0.5, tgt_f, -1.0)
    rinv_col = ccol[:, 0:1] + ccol[:, 1:2] + ccol[:, 2:3]
    share = valid_row / count
    ROWS[...] = jnp.concatenate([rinv_row, share, tgt_f, valid_row, jnp.zeros((4, CAP), F32)], axis=0)

    for k in range(1, 8):
        j = dp_from[k - 1]
        rcopy(H.at[j, ohalf, :], H.at[j, ohalf, :], HC0 + k, core_dev).wait_recv()
    hcomp = jnp.dot(S[...], H[...].reshape(8 * B, W), preferred_element_type=F32)
    C[...] = ((hcomp * rinv_col) * gain_row).astype(BF16)
    HCT[...] = jnp.transpose(hcomp)
    STAT[...] = jnp.concatenate([jnp.full((1, CAP), LOW, F32), jnp.zeros((7, CAP), F32)], axis=0)

    def order(c):
        odd = c % 2
        first = p1 * (1 - odd) + p2 * odd
        second = p2 * (1 - odd) + p1 * odd
        dev1 = (ya * (1 - odd) + yb * odd) * 2 + xh
        dev2 = (yb * (1 - odd) + ya * odd) * 2 + xh
        return first, second, (dev1, seq), (dev2, seq)

    def rows_at(start, size):
        return pl.ds(pl.multiple_of(start, 16), size)

    xdev = (xpeer, seq)

    def s1(c):
        f, g, dev1, dev2 = order(c)
        return rcopy(L.at[c, rows_at((1 - f) * 192, 192), :], R1.at[c], S10 + c, dev1)

    def s2(c):
        f, g, dev1, dev2 = order(c)
        return rcopy(A1.at[c, rows_at((1 - g) * 96, 96), :], R2.at[c], S20 + c, dev2)

    def sx(c):
        return rcopy(A2.at[c, rows_at((1 - xh) * 48, 48), :], R3.at[c], SX0 + c, xdev)

    def piece(c):
        f, g, dev1, dev2 = order(c)
        return f * 192 + g * 96 + xh * 48

    def marks(c):
        local = c * R + piece(c) + lax.broadcasted_iota(jnp.int32, (48, CAP), 0)
        inside = local < V
        hit = jnp.logical_and(inside, (local + seq * V) == ROWS[2:3, :].astype(jnp.int32))
        return inside, hit

    LAG1, LAG2, LAG3 = 2, 4, 6

    @pl.loop(0, CH + LAG3)
    def _(k):
        @pl.when(k < CH)
        def _():
            rows = pl.ds(pl.multiple_of(k * R, R), R)
            L[k] = lax.dot_general(wgt[rows, :], C[...], NT, preferred_element_type=F32).astype(BF16)
            s1(k).start()

        @pl.when(jnp.logical_and(k >= LAG1, k < CH + LAG1))
        def _():
            c = k - LAG1
            f, g, dev1, dev2 = order(c)
            s1(c).wait_recv()
            A1[c] = (L[c, rows_at(f * 192, 192), :].astype(F32) + R1[c].astype(F32)).astype(BF16)
            s2(c).start()

        @pl.when(jnp.logical_and(k >= LAG2, k < CH + LAG2))
        def _():
            c = k - LAG2
            f, g, dev1, dev2 = order(c)
            s2(c).wait_recv()
            A2[c] = (A1[c, rows_at(g * 96, 96), :].astype(F32) + R2[c].astype(F32)).astype(BF16)
            sx(c).start()

        @pl.when(k >= LAG3)
        def _():
            c = k - LAG3
            sx(c).wait_recv()
            logits = A2[c, rows_at(xh * 48, 48), :].astype(F32) + R3[c].astype(F32)
            inside, hit = marks(c)
            logits = jnp.where(inside, logits, LOW)
            F[c] = logits
            old = STAT[0:1, :]
            top = jnp.maximum(old, jnp.max(logits, axis=0, keepdims=True))
            ex = jnp.where(inside, jnp.exp(logits - top), 0.0)
            scale = jnp.exp(old - top)
            STAT[1:2, :] = STAT[1:2, :] * scale + jnp.sum(ex, axis=0, keepdims=True)
            STAT[2:3, :] = STAT[2:3, :] * scale + jnp.sum(ex * logits, axis=0, keepdims=True)
            STAT[3:4, :] = STAT[3:4, :] + jnp.sum(jnp.where(hit, logits, 0.0), axis=0, keepdims=True)
            STAT[0:1, :] = top

    def merge(slots, n):
        parts = [slots[i] for i in range(n)]
        top = parts[0][0:1, :]
        for q in parts[1:]:
            top = jnp.maximum(top, q[0:1, :])
        ssum = jnp.zeros((1, CAP), F32)
        esum = jnp.zeros((1, CAP), F32)
        tsum = jnp.zeros((1, CAP), F32)
        for q in parts:
            w = jnp.exp(q[0:1, :] - top)
            ssum = ssum + q[1:2, :] * w
            esum = esum + q[2:3, :] * w
            tsum = tsum + q[3:4, :]
        return top, ssum, esum, tsum

    def packed(vals):
        return jnp.concatenate(list(vals) + [jnp.zeros((4, CAP), F32)], axis=0)

    sends = []

    def spread(slots, mine, devs, froms, sem):
        for k, dev in enumerate(devs, 1):
            c = rcopy(slots.at[mine], slots.at[mine], sem + k, dev)
            c.start()
            sends.append(c)
        for k, src in enumerate(froms, 1):
            rcopy(slots.at[src], slots.at[src], sem + k, (dp, seq)).wait_recv()

    ST1[g_me] = STAT[...]
    spread(ST1, g_me, [(dp, z * 4 + g) for g in g_peers], g_from, T10)
    ST2[z] = packed(merge(ST1, 4))
    spread(ST2, z, [(dp, seq_of(zz, xl, co)) for zz in z_peers], z_from, T20)
    ST3[dp] = packed(merge(ST2, 8))
    spread(ST3, dp, [(j, seq) for j in dp_peers], dp_from, T30)
    top, ssum, esum, tsum = merge(ST3, 8)
    share = ROWS[1:2, :]
    valid_row = ROWS[3:4, :]
    log_total = jnp.log(ssum) + top
    loss = jnp.sum(jnp.where(valid_row > 0.5, log_total - tsum, 0.0), axis=1, keepdims=True) / count
    peak = jnp.where(valid_row > 0.5, (1.0 + jnp.abs(top)) / ssum, 0.0)
    worst = jnp.max(peak, axis=1, keepdims=True)
    wide = jnp.where(count > CAP + 0.5, 1.0, 0.0)
    other = jnp.where(worst > 0.25, 1.0, 0.0)
    scal[...] = jnp.concatenate([
        jnp.broadcast_to(loss, (1, B)), jnp.broadcast_to(jnp.maximum(wide, other), (1, B)),
        jnp.zeros((6, B), F32)], axis=0)
    ROWS[4:5, :] = top
    ROWS[5:6, :] = share / ssum
    ROWS[6:7, :] = (esum / ssum - tsum) * share * (1.0 / D)
    DN[...] = jnp.zeros_like(DN)

    def gx(c):
        me = rows_at(piece(c), 48)
        return rcopy(DL.at[c, me, :], DL.at[c, me, :], GX0 + c, xdev)

    def gx_in(c):
        f, g, dev1, dev2 = order(c)
        at = rows_at(f * 192 + g * 96 + (1 - xh) * 48, 48)
        return rcopy(DL.at[c, at, :], DL.at[c, at, :], GX0 + c, xdev)

    def g2(c):
        f, g, dev1, dev2 = order(c)
        me = rows_at(f * 192 + g * 96, 96)
        return rcopy(DL.at[c, me, :], DL.at[c, me, :], G20 + c, dev2)

    def g2_in(c):
        f, g, dev1, dev2 = order(c)
        at = rows_at(f * 192 + (1 - g) * 96, 96)
        return rcopy(DL.at[c, at, :], DL.at[c, at, :], G20 + c, dev2)

    def g1(c):
        f, g, dev1, dev2 = order(c)
        me = rows_at(f * 192, 192)
        return rcopy(DL.at[c, me, :], DL.at[c, me, :], G10 + c, dev1)

    def g1_in(c):
        f, g, dev1, dev2 = order(c)
        at = rows_at((1 - f) * 192, 192)
        return rcopy(DL.at[c, at, :], DL.at[c, at, :], G10 + c, dev1)

    @pl.loop(0, CH)
    def _(c):
        inside, hit = marks(c)
        probs = jnp.exp(F[c] - ROWS[4:5, :]) * ROWS[5:6, :]
        DL[c, rows_at(piece(c), 48), :] = (probs - jnp.where(hit, ROWS[1:2, :], 0.0)).astype(BF16)
        gx(c).start()

    K2, K3 = 2, 4

    @pl.loop(0, CH + K3)
    def _(k):
        @pl.when(k < CH)
        def _():
            gx_in(k).wait_recv()
            g2(k).start()

        @pl.when(jnp.logical_and(k >= K2, k < CH + K2))
        def _():
            c = k - K2
            g2_in(c).wait_recv()
            g1(c).start()

        @pl.when(k >= K3)
        def _():
            c = k - K3
            g1_in(c).wait_recv()
            DN[...] += jnp.dot(WT[c], DL[c], preferred_element_type=F32)

    def grad_chunk(c):
        GH[c] = lax.dot_general(DL[c], C[...], (((1,), (0,)), ((), ())), preferred_element_type=F32)

    def head_copy(c):
        n = R if c < CH - 1 else V - R * (CH - 1)
        return pltpu.make_async_copy(GH.at[c, pl.ds(0, n), :], gh.at[pl.ds(c * R, n), :], ls.at[c])

    dc = rcopy(DN.at[rows_at((1 - co) * 256, 256), :], RC, DC0, core_dev)
    dc.start()
    grad_chunk(0)
    head_copy(0).start()
    dc.wait_recv()
    T1[...] = DN[rows_at(co * 256, 256), :] + RC[...]
    B1[...] = T1[rows_at((1 - xl) * 128, 128), :].astype(BF16)
    dx = rcopy(B1, RX, DX0, xlo_dev)
    dx.start()
    for c in (1, 2, 3):
        grad_chunk(c)
        head_copy(c).start()
    dx.wait_recv()
    T2[...] = T1[rows_at(xl * 128, 128), :] + RX[...].astype(F32)
    for i in range(8):
        B2[i] = T2[i * 16:(i + 1) * 16, :].astype(BF16)
    dz = []
    for k in range(1, 8):
        c = rcopy(B2.at[z_peers[k - 1]], RZ.at[z], DZ0 + k, (dp, seq_of(z_peers[k - 1], xl, co)))
        c.start()
        dz.append(c)
    for c in (4, 5, 6):
        grad_chunk(c)
        head_copy(c).start()
    for k in range(1, 8):
        rcopy(RZ.at[z_from[k - 1]], RZ.at[z_from[k - 1]], DZ0 + k, (dp, seq)).wait_recv()
    dn = T2[rows_at(z * 16, 16), :]
    for k in range(1, 8):
        dn = dn + RZ[z_from[k - 1]].astype(F32)

    off = co * 256 + xl * 128 + z * 16
    rinv_row = ROWS[0:1, :]
    xn = HCT[rows_at(off, 16), :] * rinv_row
    gc = GCOL[rows_at(off, 16), 0:1]
    grow = (rinv_row * (dn * gc - xn * ROWS[6:7, :])).astype(BF16)
    ggc = jnp.sum(dn * xn, axis=1, keepdims=True)
    wide_rows = jnp.dot(grow, S[...], preferred_element_type=F32).astype(BF16)
    ghi = ggc.astype(BF16).astype(F32)
    gmid = (ggc - ghi).astype(BF16).astype(F32)
    glo = (ggc - ghi) - gmid
    lane = lax.broadcasted_iota(jnp.int32, (16, B), 1)
    gparts = jnp.where(lane == 0, ghi, jnp.where(lane == 1, gmid, jnp.where(lane == 2, glo, 0.0))).astype(BF16)
    for j in range(8):
        MB[j, 0:16, :] = wide_rows[:, j * B:(j + 1) * B]
        MB[j, 16:32, :] = gparts
    dpc = []
    for k in range(1, 8):
        c = rcopy(MB.at[dp_peers[k - 1]], RB.at[dp], DP0 + k, (dp_peers[k - 1], seq))
        c.start()
        dpc.append(c)
    RB[dp] = MB[dp]
    for k in range(1, 8):
        rcopy(RB.at[dp_from[k - 1]], RB.at[dp_from[k - 1]], DP0 + k, (dp, seq)).wait_recv()

    mine = rows_at(off, 16)
    for j in range(8):
        GT[j, mine, :] = RB[j, 0:16, :]
    gsum = jnp.transpose(RB[:, 16:32, :].reshape(B, B).astype(F32))
    grow1 = gsum[0:1, :] + gsum[1:2, :] + gsum[2:3, :]
    gidx = co * 16 + xl * 8 + z
    GG[gidx] = jnp.broadcast_to(grow1, (8, B))
    for k in range(1, 8):
        dev = (dp, seq_of(z_peers[k - 1], xl, co))
        c = rcopy(GT.at[:, mine, :], GT.at[:, mine, :], AZ0 + k, dev)
        c.start()
        sends.append(c)
        c = rcopy(GG.at[gidx], GG.at[gidx], BZ0 + k, dev)
        c.start()
        sends.append(c)
    for k in range(1, 8):
        zf = z_from[k - 1]
        at = rows_at(co * 256 + xl * 128 + zf * 16, 16)
        rcopy(GT.at[:, at, :], GT.at[:, at, :], AZ0 + k, (dp, seq)).wait_recv()
        gi = co * 16 + xl * 8 + zf
        rcopy(GG.at[gi], GG.at[gi], BZ0 + k, (dp, seq)).wait_recv()

    def step(start, size, gstart, gsize, ostart, ogstart, sa, sb, dev):
        a = rcopy(GT.at[:, rows_at(start, size), :], GT.at[:, rows_at(start, size), :], sa, dev)
        b = rcopy(GG.at[pl.ds(gstart, gsize)], GG.at[pl.ds(gstart, gsize)], sb, dev)
        a.start()
        b.start()
        sends.append(a)
        sends.append(b)
        rcopy(GT.at[:, rows_at(ostart, size), :], GT.at[:, rows_at(ostart, size), :], sa, dev).wait_recv()
        rcopy(GG.at[pl.ds(ogstart, gsize)], GG.at[pl.ds(ogstart, gsize)], sb, dev).wait_recv()

    step(co * 256 + xl * 128, 128, co * 16 + xl * 8, 8,
         co * 256 + (1 - xl) * 128, co * 16 + (1 - xl) * 8, AX0, BX0, xlo_dev)
    step(co * 256, 256, co * 16, 16, (1 - co) * 256, (1 - co) * 16, AC0, BC0, core_dev)
    for j in range(8):
        for b in range(4):
            ghid[:, j * W + b * B:j * W + (b + 1) * B] = jnp.transpose(GT[j, b * B:(b + 1) * B, :])
    gg[...] = GG[:, 0, :]

    for c in hsend + msend + hc + sends + [dc, dx] + dz + dpc:
        c.wait_send()

    @pl.loop(0, CH)
    def _(c):
        s1(c).wait_send()
        s2(c).wait_send()
        sx(c).wait_send()
        gx(c).wait_send()
        g2(c).wait_send()
        g1(c).wait_send()
    for c in range(CH):
        head_copy(c).wait()


def fused(hidden, gain, head_weight, targets, loss_mask):
    wgt = jnp.pad(head_weight, ((0, CH * R - V), (0, 0)))
    vm = pl.BlockSpec(memory_space=pltpu.VMEM)
    scratch = [
        pltpu.VMEM((8, B, W), BF16),
        pltpu.VMEM((8, 8, B), F32),
        pltpu.VMEM((CH, W, R), BF16),
        pltpu.VMEM((CAP, 8 * B), BF16),
        pltpu.VMEM((8, 128), F32),
        pltpu.VMEM((W, CAP), F32),
        pltpu.VMEM((CAP, W), BF16),
        pltpu.VMEM((W, B), F32),
        pltpu.VMEM((8, CAP), F32),
        pltpu.VMEM((CH, R, CAP), BF16),
        pltpu.VMEM((CH, 192, CAP), BF16),
        pltpu.VMEM((CH, 192, CAP), BF16),
        pltpu.VMEM((CH, 96, CAP), BF16),
        pltpu.VMEM((CH, 96, CAP), BF16),
        pltpu.VMEM((CH, 48, CAP), BF16),
        pltpu.VMEM((CH, 48, CAP), F32),
        pltpu.VMEM((8, CAP), F32),
        pltpu.VMEM((4, 8, CAP), F32),
        pltpu.VMEM((8, 8, CAP), F32),
        pltpu.VMEM((8, 8, CAP), F32),
        pltpu.VMEM((CH, R, CAP), BF16),
        pltpu.VMEM((W, CAP), F32),
        pltpu.VMEM((256, CAP), F32),
        pltpu.VMEM((256, CAP), F32),
        pltpu.VMEM((128, CAP), BF16),
        pltpu.VMEM((128, CAP), BF16),
        pltpu.VMEM((128, CAP), F32),
        pltpu.VMEM((8, 16, CAP), BF16),
        pltpu.VMEM((8, 16, CAP), BF16),
        pltpu.VMEM((8, 32, B), BF16),
        pltpu.VMEM((8, 32, B), BF16),
        pltpu.VMEM((8, W, B), BF16),
        pltpu.VMEM((32, 8, B), F32),
        pltpu.VMEM((CH, R, W), F32),
        pltpu.SemaphoreType.DMA((NSEM,)),
        pltpu.SemaphoreType.DMA((NSEM,)),
        pltpu.SemaphoreType.DMA((CH,)),
    ]
    gh, ghid, gg, scal = pl.pallas_call(
        kernel,
        out_shape=(
            jax.ShapeDtypeStruct((V, W), F32),
            jax.ShapeDtypeStruct((B, D), BF16),
            jax.ShapeDtypeStruct((32, B), F32),
            jax.ShapeDtypeStruct((8, B), F32),
        ),
        in_specs=[vm] * 5,
        out_specs=(pl.BlockSpec(memory_space=pl.ANY), vm, vm, vm),
        scratch_shapes=scratch,
        compiler_params=pltpu.CompilerParams(
            collective_id=0, has_side_effects=True, vmem_limit_bytes=56 * 1024 * 1024),
        cost_estimate=pl.CostEstimate(flops=6 * V * CAP * W, bytes_accessed=16 * 1024 * 1024, transcendentals=0),
        name="fused",
    )(hidden, gain.reshape(8, W), wgt, targets.reshape(1, B), loss_mask.reshape(1, B))
    grad_gain = jnp.transpose(gg.reshape(32, 8, 16), (1, 0, 2)).reshape(D)
    return scal, ghid, grad_gain, gh


def norm_back(grad_normed, unit_rows, inv_rms, gain):
    grad_unit = grad_normed * gain
    return inv_rms * (
        grad_unit - unit_rows * jnp.mean(grad_unit * unit_rows, axis=-1, keepdims=True)
    )


def general(hidden, gain, head_weight, targets, loss_mask):
    floats = hidden.astype(jnp.float32)
    inv_rms = lax.rsqrt(jnp.mean(floats * floats, axis=-1, keepdims=True) + EPS)
    unit_rows = floats * inv_rms
    normed = (unit_rows * gain).astype(jnp.bfloat16)
    mask_float = loss_mask.astype(jnp.float32)
    num_valid = lax.psum(jnp.sum(mask_float), "dp")
    slices = lax.all_to_all(normed, "dp", split_axis=1, concat_axis=0, tiled=True)
    vocab_rows = head_weight.shape[0]
    logits = lax.psum_scatter(
        lax.dot_general(slices, head_weight, NT, preferred_element_type=jnp.float32),
        "dp",
        scatter_dimension=0,
        tiled=True,
    )
    column = lax.axis_index("seq") * vocab_rows + jnp.arange(vocab_rows, dtype=jnp.int32)
    one_hot = (column[None, :] == targets[:, None]).astype(jnp.float32)
    local_picked = jnp.sum(one_hot * logits, axis=1)
    row_top = lax.pmax(jnp.max(logits, axis=1), "seq")
    shifted = jnp.exp(logits - row_top[:, None])
    row_total, picked = lax.psum((jnp.sum(shifted, axis=1), local_picked), "seq")
    log_total = row_top + jnp.log(row_total)
    probs = shifted / row_total[:, None]
    row_loss = log_total - picked
    loss_value = lax.psum(jnp.sum(mask_float * row_loss), "dp") / num_valid
    dlogits = ((probs - one_hot) * (mask_float / num_valid)[:, None]).astype(jnp.bfloat16)
    shard_rows = lax.all_gather(dlogits, "dp", axis=0, tiled=True)
    grad_slices = jnp.dot(shard_rows, head_weight, preferred_element_type=jnp.float32)
    grad_head = lax.dot_general(
        shard_rows, slices, (((0,), (0,)), ((), ())), preferred_element_type=jnp.float32
    )
    returned = lax.all_to_all(grad_slices, "dp", split_axis=0, concat_axis=1, tiled=True)
    grad_normed = lax.psum(returned, "seq")
    grad_gain = lax.psum(jnp.sum(grad_normed * unit_rows, axis=0), "dp")
    grad_hidden = norm_back(grad_normed, unit_rows, inv_rms, gain).astype(jnp.bfloat16)
    return (loss_value, grad_hidden, grad_gain, grad_head)


def body(hidden, gain, head_weight, targets, loss_mask):
    scal, grad_hidden, grad_gain, grad_head = fused(hidden, gain, head_weight, targets, loss_mask)

    def keep(*args):
        return scal[0, 0], grad_hidden, grad_gain, grad_head

    return lax.cond(scal[1, 0] > 0.5, general, keep, hidden, gain, head_weight, targets, loss_mask)


def solution(mesh):
    return jax.shard_map(
        body,
        mesh=mesh,
        in_specs=(P("dp", None), P(), P("seq", "dp"), P("dp"), P("dp")),
        out_specs=(P(), P("dp", None), P(), P("seq", "dp")),
        check_vma=False,
    )
```

time: 740 us -> 888 us (1.20)
  Pallas kernels: 0 us -> 148 us
    pallas_call x0 -> x1, Pallas kernels: none -> 148 us  [fused(): pl.pallas_call(kernel, out_shape=(jax.ShapeDtypeStruct((V, W), F32), jax....]
where the time goes in v1:
time: 888 us
  waiting for transfers between devices  447 us (50%)
  blocking collectives  227 us (26%)
  Pallas kernels  148 us (17%)
  matrix products  21 us (2%)
  local copies, waits for them, and re-layouts  16.8 us (2%)
  between operations  14.4 us (2%)
  other arithmetic  11.9 us (1%)
    psum x1, waiting for transfers between devices, general(): grad_normed = lax.psum(returned, 'seq')  219 us
    pallas_call x1, Pallas kernels, fused(): pl.pallas_call(kernel, out_shape=(jax.ShapeDtypeStruct((V, W), F32), jax....  148 us
    reduce_scatter x1, waiting for transfers between devices, general(): lax.psum_scatter(lax.dot_general(slices, head_weight, NT, preferred_eleme...  143 us
    all_gather x1, waiting for transfers between devices, general(): shard_rows = lax.all_gather(dlogits, 'dp', axis=0, tiled=True)  85 us
    pmax x1, blocking collectives, general(): row_top = lax.pmax(jnp.max(logits, axis=1), 'seq')  55.2 us
    psum x1, blocking collectives, general(): lax.psum((jnp.sum(shifted, axis=1), local_picked), 'seq')  53 us
    psum x1, blocking collectives, general(): loss_value = lax.psum(jnp.sum(mask_float * row_loss), 'dp') / num_valid  43 us
    all_to_all x1, blocking collectives, general(): lax.all_to_all(grad_slices, 'dp', split_axis=0, concat_axis=1, tiled=True)  30.8 us
  transfers between devices with their start and end apart: 3, of which 3 were waited for; matrix products, arithmetic and copies ran while one was open for 1% of the time, Pallas kernels for 0%

profile of v1, /device:TPU:0, one launch (start us, length us, event | category | flops | bytes accessed | tf_op | source)
XLA Modules:
  0.0 887.8 jit_solution(15273447217984369423)
XLA Ops:
  7.2 0.0 copy-start.5
  7.2 0.0 copy-start.6
  7.2 0.0 copy-start.7
  7.2 0.0 copy-start.2
  7.2 3.6 pad.4.wgt
  10.8 0.0 copy-done.5
  10.8 0.6 reshape.55.gain
  11.4 0.0 copy-done.6
  11.4 0.0 copy-done.7
  11.4 147.6 %fused.1 = (f32[2632,512]{1,0:T(8,128)}, bf16[128,4096]{1,0:T(8,128)(2,1)S(1)}, f32[32,128]{1,0:T(8,128)}, f32[8,128]{1,0:T(8,128)S(1)}) custom-call(bf16[128,4096]{1,0:T(8,128)(2,1)S(1)} %copy-done.2, f32[8,512]{1,0:T(8,128)} %reshape.55.gain, bf16[2688,512]{1,0:T(8,128)(2,1)} %pad.4.wgt, s32[1,128]{1,0:T(1,128)S(1)} %bitcast.27, s32[1,128]{1,0:T(1,128)S(1)} %bitcast.28), custom_call_target="tpu_custom_call" | custom-call | flops 5174722560 | bytes 16777216 | tf_op jit(solution)/shard_map/fused/pallas_call | solution.py:491
  159.0 0.8 copy.20
  159.8 0.5 slice.6
  161.0 713.8 %conditional.1 = (f32[2632,512]{1,0:T(8,128)}, f32[]{:T(128)}, f32[4096]{0:T(1024)}, bf16[128,4096]{1,0:T(8,128)(2,1)S(1)}) conditional(s32[]{:T(128)} %bitcast.9, (f32[8,128]{1,0:T(8,128)S(1)}, f32[8,32,16]{1,2,0:T(8,128)S(1)}, bf16[128,4096]{1,0:T(8,128)(2,1)S(1)}, f32[2632,512]{1,0:T(8,128)}) %tuple.42, (s32[128]{0:T(128)S(1)}, ...), branch_computations={%region_0.1_spmd, %region_1.18_spmd} | conditional | flops 8295473664 | bytes 157989536 | solution.py:562
  161.0 0.0 reduce-scatter.2.cloned.1.call-start
  161.1 0.7 copy.23
  161.7 0.6 fusion.10
  162.3 0.7 fusion.4
  163.0 22.8 %all_to_all.30 = bf16[128,8,512]{0,2,1:T(8,128)(2,1)S(1)} all-to-all(bf16[128,8,512]{0,2,1:T(8,128)(2,1)S(1)} %bitcast.21), channel_id=1, replica_groups=mesh['dp'=8,'seq'=32] {'dp'}, dimensions={1} | all-to-all | bytes 2097152 | tf_op jit(solution)/shard_map/cond/branch_1_fun/all_to_all | solution.py:525
  185.8 0.5 copy.18
  186.4 0.0 copy-start.3
  186.4 7.8 fusion.16
  194.2 0.0 reduce-scatter.2.cloned.1.call-update
  194.2 0.0 all-gather.2.cloned.1.call-start
  194.3 143.0 %reduce-scatter.2.cloned.1.call-done = f32[128,2632]{0,1:T(8,128)} async-done(((f32[1024,2632]{0,1:T(8,128)}), f32[128,2632]{0,1:T(8,128)}) %reduce-scatter.2.cloned.1.call-update) | async-done | bytes 1347600 | tf_op jit(solution)/shard_map/cond/branch_1_fun/reduce_scatter | solution.py:527
  337.3 1.8 reduce_max.8
  339.1 55.2 %pmax.6 = f32[128]{0:T(128)S(1)} all-reduce(f32[128]{0:T(128)S(1)} %reduce_max.8), channel_id=1, replica_groups=mesh['dp'=8,'seq'=32] {'seq'}, use_global_device_ids=true, to_apply=%region_5.5 | all-reduce | flops 128 | bytes 1024 | tf_op jit(solution)/shard_map/cond/branch_1_fun/pmax | solution.py:536
  394.3 2.3 fusion.11
  396.6 53.0 %all-reduce.1 = (f32[128]{0:T(128)S(1)}, f32[128]{0:T(128)S(1)}) all-reduce(f32[128]{0:T(128)S(1)} %get-tuple-element.62, f32[128]{0:T(128)S(1)} %get-tuple-element.63), channel_id=1, replica_groups=mesh['dp'=8,'seq'=32] {'seq'}, use_global_device_ids=true, to_apply=%region_9.9 | all-reduce | flops 256 | bytes 2048 | tf_op jit(solution)/shard_map/cond/branch_1_fun/psum | solution.py:538
  449.5 0.6 multiply_reduce_fusion
  450.2 22.2 %psum.39 = f32[]{:T(128)} all-reduce(f32[]{:T(128)} %get-tuple-element.65), channel_id=1, replica_groups=mesh['dp'=8,'seq'=32] {'dp'}, use_global_device_ids=true, to_apply=%region_13.13 | all-reduce | flops 1 | bytes 8 | tf_op jit(solution)/shard_map/cond/branch_1_fun/psum | solution.py:524
  472.3 0.6 convert_divide_fusion
  472.9 2.0 fusion.14
  474.8 0.0 all-gather.2.cloned.1.call-update
  474.9 0.0 all-reduce.5.cloned.1.call-start
  474.9 85.0 %all-gather.2.cloned.1.call-done = bf16[1024,2632]{0,1:T(8,128)(2,1)} async-done(((bf16[128,2632]{0,1:T(8,128)(2,1)}), bf16[1024,2632]{0,1:T(8,128)(2,1)}) %all-gather.2.cloned.1.call-update) | async-done | bytes 5390352 | tf_op jit(solution)/shard_map/cond/branch_1_fun/all_gather | solution.py:544
  559.9 6.0 fusion.17
  565.9 30.8 %all_to_all.31 = f32[8,128,512]{2,1,0:T(8,128)S(1)} all-to-all(f32[8,128,512]{2,1,0:T(8,128)S(1)} %bitcast.23), channel_id=1, replica_groups=mesh['dp'=8,'seq'=32] {'dp'}, dimensions={0} | all-to-all | bytes 4194304 | tf_op jit(solution)/shard_map/cond/branch_1_fun/all_to_all | solution.py:549
  596.6 1.8 copy.19
  598.4 0.0 all-reduce.5.cloned.1.call-update
  598.4 1.2 copy-done.4
  599.6 7.2 fusion.18
  606.9 219.2 %all-reduce.5.cloned.1.call-done = f32[128,4096]{0,1:T(8,128)} async-done(((f32[128,4096]{0,1:T(8,128)}), f32[128,4096]{0,1:T(8,128)}) %all-reduce.5.cloned.1.call-update) | async-done | bytes 2097168 | tf_op jit(solution)/shard_map/cond/branch_1_fun/psum | solution.py:550
  826.1 2.6 fusion.5
  828.8 0.7 fusion.8
  829.5 0.5 copy.26
  830.1 43.0 %all-reduce.2 = (f32[]{:T(128)}, f32[4096]{0:T(1024)}) all-reduce(f32[]{:T(128)} %get-tuple-element.64, f32[4096]{0:T(1024)S(1)} %get-tuple-element.61), channel_id=1, replica_groups=mesh['dp'=8,'seq'=32] {'dp'}, use_global_device_ids=true, to_apply=%region_11.11 | all-reduce | flops 4097 | bytes 32776 | tf_op jit(solution)/shard_map/cond/branch_1_fun/psum | solution.py:542
  874.8 1.0 copy.38
  875.8 5.5 copy.39
  (10 shorter events, 0.0 us)
Async XLA Ops:
  7.2 3.6 copy-start.5
  7.2 4.2 copy-start.6
  7.2 4.2 copy-start.7
  7.2 4.2 copy-start.2
  161.0 176.3 %reduce-scatter.2.cloned.1.call-start = ((), (), s32[]{:S(2)}) async-start(), calls=%async_computation.3 | async-start | bytes 12128256 | tf_op jit(solution)/shard_map/cond/branch_1_fun/reduce_scatter | solution.py:527
  186.4 7.9 copy-start.3
  194.2 365.6 %all-gather.2.cloned.1.call-start = ((), (), s32[]{:S(2)}) async-start(), calls=%async_computation.4 | async-start | bytes 6064128 | tf_op jit(solution)/shard_map/cond/branch_1_fun/all_gather | solution.py:544
  337.3 135.6 %copy-start = (f32[128,2632]{0,1:T(8,128)S(1)}, f32[128,2632]{0,1:T(8,128)}, u32[]{:S(2)}) copy-start(f32[128,2632]{0,1:T(8,128)} %reduce-scatter.2.cloned.1.call-done) | copy-start | bytes 4042756 | tf_op jit(solution)/shard_map/cond
  474.9 351.2 %all-reduce.5.cloned.1.call-start = ((), (), s32[]{:S(2)}) async-start(), calls=%async_computation.5 | async-start | bytes 4194304 | tf_op jit(solution)/shard_map/cond/branch_1_fun/psum | solution.py:550
  598.4 1.2 copy-start.4
  826.1 2.7 copy-start.1
Sparse Core Ops, SparseCore 0:
  194.4 142.8 reduce-scatter.1
  475.0 84.8 all-gather.1
  598.6 227.5 all-reduce.4

commit v2 on v0

v2 whole, which is shorter than its diff:
```python
import jax
import jax.numpy as jnp
from jax import lax
from jax.experimental import pallas as pl
from jax.experimental.pallas import tpu as pltpu
from jax.sharding import PartitionSpec as P

EPS = 1e-05
MESH = pl.DeviceIdType.MESH
F32 = jnp.float32
BF16 = jnp.bfloat16
NT = (((1,), (1,)), ((), ()))

D = 4096
W = 512
B = 128
V = 2632
VP = 2688
CAP = 640
CH = 7
R = VP // CH
RH, RQ, RP = R // 2, R // 4, R // 8
G = 384
LOW = -1e30

LAG1, LAG2, LAG3, LAG4, LAG5 = 2, 3, 4, 6, 8

NSEM = 0


def sems(n):
    global NSEM
    NSEM += n
    return NSEM - n


H0, M0, HC0 = sems(8), sems(8), sems(8)
S10, S20, S30, G30, G20, G10 = [sems(CH) for _ in range(6)]
T10, T20, T30 = sems(4), sems(8), sems(8)
DC0, DX0, DZ0, DP0, AZ0, AX0, AC0 = sems(1), sems(8), sems(8), sems(8), sems(8), sems(8), sems(2)


def kernel(hid, gain, wgt, tgt, msk, dlo, C, GTX, scal, flag,
           H, META, WP, WT, S, HCT, GCOL, ROWS, L, R1, A1, R2, A2, R3, STAT, ST1, ST2, ST3,
           PR, DN, RC, T1, B1, RX, B2, RZ, MB, RB, ss, rs):
    dp = lax.axis_index("dp")
    seq = lax.axis_index("seq")
    y, xh = dp // 2, dp % 2
    z, xl, co = seq // 4, (seq // 2) % 2, seq % 2
    p1, p2 = (y // 2 + y) % 2, y // 2
    ya, yb = (y + 1 - 2 * (y % 2)) * 2 + xh, (3 - y) * 2 + xh
    xpeer = y * 2 + 1 - xh

    def seq_of(zz, xx, cc):
        return zz * 4 + xx * 2 + cc

    def rcopy(src, dst, sem, dev):
        return pltpu.make_async_remote_copy(
            src_ref=src, dst_ref=dst, send_sem=ss.at[sem], recv_sem=rs.at[sem],
            device_id=dev, device_id_type=MESH)

    def rows_at(start, size):
        return pl.ds(pl.multiple_of(start, 16), size)

    dp_peers = [lax.rem(dp + k, 8) for k in range(1, 8)]
    dp_from = [lax.rem(dp + 8 - k, 8) for k in range(1, 8)]
    z_peers = [lax.rem(z + k, 8) for k in range(1, 8)]
    z_from = [lax.rem(z + 8 - k, 8) for k in range(1, 8)]
    g_me = xl * 2 + co
    g_peers = [lax.rem(g_me + k, 4) for k in range(1, 4)]
    g_from = [lax.rem(g_me + 4 - k, 4) for k in range(1, 4)]
    core_dev = (dp, seq_of(z, xl, 1 - co))
    xlo_dev = (dp, seq_of(z, 1 - xl, co))

    barrier = pltpu.get_barrier_semaphore()
    for j in dp_peers:
        pl.semaphore_signal(barrier, inc=1, device_id=(j, seq), device_id_type=MESH)
    for g in g_peers:
        pl.semaphore_signal(barrier, inc=1, device_id=(dp, z * 4 + g), device_id_type=MESH)
    for zz in z_peers:
        pl.semaphore_signal(barrier, inc=1, device_id=(dp, seq_of(zz, xl, co)), device_id_type=MESH)

    total = jnp.zeros((B, 1), F32)
    for j in range(8):
        x = hid[:, j * W:(j + 1) * W].astype(F32)
        total = total + jnp.sum(x * x, axis=1, keepdims=True)
    rinv = lax.rsqrt(total * (1.0 / D) + EPS)
    rinv_t = jnp.transpose(jnp.broadcast_to(rinv, (B, B)))
    META[dp] = jnp.concatenate(
        [rinv_t[0:1, :], msk[...].astype(F32), tgt[...].astype(F32), jnp.zeros((5, B), F32)], axis=0)
    H[dp] = hid[:, pl.ds(pl.multiple_of(dp * W, W), W)]
    pl.semaphore_wait(barrier, 17)

    half = pl.ds(pl.multiple_of(co * 64, 64), 64)
    ohalf = pl.ds(pl.multiple_of((1 - co) * 64, 64), 64)
    hsend = []
    msend = []
    for k in range(1, 8):
        j = dp_peers[k - 1]
        c = rcopy(META.at[dp], META.at[dp], M0 + k, (j, seq))
        c.start()
        msend.append(c)
        c = rcopy(hid.at[half, pl.ds(pl.multiple_of(j * W, W), W)], H.at[dp, half, :], H0 + k, (j, seq))
        c.start()
        hsend.append(c)

    for i in range(6):
        WP[i * G:(i + 1) * G, :] = wgt[i * G:(i + 1) * G, :]
    WP[6 * G:V - 8, :] = wgt[6 * G:V - 8, :]
    WP[V - 8:V + 8, :] = jnp.concatenate(
        [wgt[V - 8:V, :].astype(F32), jnp.zeros((8, W), F32)], axis=0).astype(BF16)
    WP[V + 8:VP, :] = jnp.zeros((VP - V - 8, W), BF16)
    gain_row = jnp.concatenate([gain[pl.ds(dp * 4 + i, 1), :] for i in range(4)], axis=1)
    GCOL[...] = jnp.transpose(jnp.broadcast_to(gain_row, (B, W)))
    STAT[...] = jnp.concatenate([jnp.full((1, CAP), LOW, F32), jnp.zeros((7, CAP), F32)], axis=0)
    DN[...] = jnp.zeros_like(DN)

    for k in range(1, 8):
        j = dp_from[k - 1]
        rcopy(META.at[j], META.at[j], M0 + k, (dp, seq)).wait_recv()
    metas = [META[j] for j in range(8)]
    m8 = jnp.concatenate([m[1:2, :] for m in metas] + [jnp.zeros((8, B), F32)], axis=0)
    tri = (lax.broadcasted_iota(jnp.int32, (B, B), 0) <= lax.broadcasted_iota(jnp.int32, (B, B), 1)).astype(F32)
    cum = jnp.dot(m8.astype(BF16), tri.astype(BF16), preferred_element_type=F32)
    base = jnp.zeros((1, 1), F32)
    slot = lax.broadcasted_iota(jnp.int32, (CAP, B), 0)
    for j in range(8):
        rank = jnp.where(metas[j][1:2, :] > 0.5, cum[j:j + 1, :] + base - 1.0, -1.0).astype(jnp.int32)
        S[:, j * B:(j + 1) * B] = (slot == rank).astype(F32).astype(BF16)
        base = base + jnp.sum(metas[j][1:2, :], axis=1, keepdims=True)
    count = base
    r_all = jnp.concatenate([m[0:1, :] for m in metas], axis=1)
    v_all = jnp.concatenate([m[1:2, :] for m in metas], axis=1)
    t_all = jnp.concatenate([m[2:3, :] for m in metas], axis=1)
    hi = r_all.astype(BF16).astype(F32)
    mid = (r_all - hi).astype(BF16).astype(F32)
    lo = (r_all - hi) - mid
    ta = jnp.floor(t_all * (1.0 / 4096))
    tb = jnp.floor((t_all - ta * 4096) * (1.0 / 64))
    tc = t_all - ta * 4096 - tb * 64
    mr = jnp.concatenate([hi, mid, lo, v_all, ta, tb, tc, jnp.zeros((9, 8 * B), F32)], axis=0).astype(BF16)
    crow = lax.dot_general(mr, S[...], NT, preferred_element_type=F32)
    mr2 = jnp.concatenate([mr, jnp.zeros((B - 16, 8 * B), BF16)], axis=0)
    ccol = lax.dot_general(S[...], mr2, NT, preferred_element_type=F32)
    valid_row = crow[3:4, :]
    tgt_f = crow[4:5, :] * 4096.0 + crow[5:6, :] * 64.0 + crow[6:7, :] - (seq * V).astype(F32)
    here = jnp.logical_and(valid_row > 0.5, jnp.logical_and(tgt_f > -0.5, tgt_f < V - 0.5))
    tgt_f = jnp.where(here, tgt_f, -1.0)
    rinv_col = ccol[:, 0:1] + ccol[:, 1:2] + ccol[:, 2:3]
    ROWS[...] = jnp.concatenate(
        [crow[0:1, :] + crow[1:2, :] + crow[2:3, :], valid_row / count, tgt_f, valid_row,
         jnp.zeros((4, CAP), F32)], axis=0)

    hc = []
    for k in range(1, 8):
        j = dp_from[k - 1]
        rcopy(H.at[j, half, :], H.at[j, half, :], H0 + k, (dp, seq)).wait_recv()
        c = rcopy(H.at[j, half, :], H.at[j, half, :], HC0 + k, core_dev)
        c.start()
        hc.append(c)
    for k in range(1, 8):
        j = dp_from[k - 1]
        rcopy(H.at[j, ohalf, :], H.at[j, ohalf, :], HC0 + k, core_dev).wait_recv()
    hcomp = jnp.dot(S[...], H[...].reshape(8 * B, W), preferred_element_type=F32)
    C[...] = ((hcomp * rinv_col) * gain_row).astype(BF16)

    def axis(c, s):
        a = (c + s) % 3
        e0, e1, e2 = (2 - a) * (1 - a) // 2, a * (2 - a), a * (a - 1) // 2
        return p1 * e0 + p2 * e1 + xh * e2, (ya * e0 + yb * e1 + xpeer * e2, seq)

    def bits(c):
        return axis(c, 0)[0], axis(c, 1)[0], axis(c, 2)[0]

    def s1(c):
        f, g, h = bits(c)
        return rcopy(L.at[rows_at(c * R + (1 - f) * RH, RH), :], R1.at[c], S10 + c, axis(c, 0)[1])

    def s2(c):
        f, g, h = bits(c)
        return rcopy(A1.at[c, rows_at((1 - g) * RQ, RQ), :], R2.at[c], S20 + c, axis(c, 1)[1])

    def s3(c):
        f, g, h = bits(c)
        return rcopy(A2.at[c, rows_at((1 - h) * RP, RP), :], R3.at[c], S30 + c, axis(c, 2)[1])

    def within(start, size, sem, dev):
        return rcopy(PR.at[rows_at(start, size), :], PR.at[rows_at(start, size), :], sem, dev)

    def g3(c, other=0):
        f, g, h = bits(c)
        h = h + other * (1 - 2 * h)
        return within(c * R + f * RH + g * RQ + h * RP, RP, G30 + c, axis(c, 2)[1])

    def g2(c, other=0):
        f, g, h = bits(c)
        g = g + other * (1 - 2 * g)
        return within(c * R + f * RH + g * RQ, RQ, G20 + c, axis(c, 1)[1])

    def g1(c, other=0):
        f, g, h = bits(c)
        f = f + other * (1 - 2 * f)
        return within(c * R + f * RH, RH, G10 + c, axis(c, 0)[1])

    def gather_steps(k):
        @pl.when(jnp.logical_and(k >= LAG4, k < CH + LAG4))
        def _():
            g3(k - LAG4, 1).wait_recv()
            g2(k - LAG4).start()

        @pl.when(jnp.logical_and(k >= LAG5, k < CH + LAG5))
        def _():
            g2(k - LAG5, 1).wait_recv()
            g1(k - LAG5).start()

    @pl.loop(0, CH + LAG3)
    def _(k):
        @pl.when(k < CH)
        def _():
            rows = rows_at(k * R, R)
            L[rows, :] = lax.dot_general(WP[rows, :], C[...], NT, preferred_element_type=F32).astype(BF16)
            s1(k).start()

        @pl.when(jnp.logical_and(k >= LAG1, k < CH + LAG1))
        def _():
            c = k - LAG1
            f, g, h = bits(c)
            s1(c).wait_recv()
            A1[c] = (L[rows_at(c * R + f * RH, RH), :].astype(F32) + R1[c].astype(F32)).astype(BF16)
            s2(c).start()

        @pl.when(jnp.logical_and(k >= LAG2, k < CH + LAG2))
        def _():
            c = k - LAG2
            f, g, h = bits(c)
            s2(c).wait_recv()
            A2[c] = (A1[c, rows_at(g * RQ, RQ), :].astype(F32) + R2[c].astype(F32)).astype(BF16)
            s3(c).start()

        @pl.when(k >= LAG3)
        def _():
            c = k - LAG3
            f, g, h = bits(c)
            s3(c).wait_recv()
            logits = A2[c, rows_at(h * RP, RP), :].astype(F32) + R3[c].astype(F32)
            first = c * R + f * RH + g * RQ + h * RP
            local = first + lax.broadcasted_iota(jnp.int32, (RP, CAP), 0)
            inside = local < V
            ex = jnp.where(inside, jnp.exp(logits), 0.0)
            PR[rows_at(first, RP), :] = ex.astype(BF16)
            g3(c).start()
            hit = local == ROWS[2:3, :].astype(jnp.int32)
            STAT[0:1, :] = jnp.maximum(
                STAT[0:1, :], jnp.max(jnp.where(inside, logits, LOW), axis=0, keepdims=True))
            STAT[1:2, :] = STAT[1:2, :] + jnp.sum(ex, axis=0, keepdims=True)
            STAT[2:3, :] = STAT[2:3, :] + jnp.sum(ex * logits, axis=0, keepdims=True)
            STAT[3:4, :] = STAT[3:4, :] + jnp.sum(jnp.where(hit, logits, 0.0), axis=0, keepdims=True)

        gather_steps(k)

    def merge(slots, n):
        parts = [slots[i] for i in range(n)]
        top = parts[0][0:1, :]
        sums = parts[0][1:4, :]
        for q in parts[1:]:
            top = jnp.maximum(top, q[0:1, :])
            sums = sums + q[1:4, :]
        return jnp.concatenate([top, sums, jnp.zeros((4, CAP), F32)], axis=0)

    sends = []

    def spread(slots, mine, devs, sem):
        for k, dev in enumerate(devs, 1):
            c = rcopy(slots.at[mine], slots.at[mine], sem + k, dev)
            c.start()
            sends.append(c)

    def collect(slots, froms, sem):
        for k, src in enumerate(froms, 1):
            rcopy(slots.at[src], slots.at[src], sem + k, (dp, seq)).wait_recv()

    last = CH + LAG3
    mids = [last + (LAG5 - LAG3) * i // 3 for i in range(4)]
    ST1[g_me] = STAT[...]
    spread(ST1, g_me, [(dp, z * 4 + g) for g in g_peers], T10)
    HCT[...] = jnp.transpose(hcomp)

    @pl.loop(mids[0], mids[1])
    def _(k):
        gather_steps(k)
    collect(ST1, g_from, T10)
    ST2[z] = merge(ST1, 4)
    spread(ST2, z, [(dp, seq_of(zz, xl, co)) for zz in z_peers], T20)

    @pl.loop(0, VP // G)
    def _(i):
        WT[i] = jnp.transpose(WP[pl.ds(pl.multiple_of(i * G, G), G), :])

    @pl.loop(mids[1], mids[2])
    def _(k):
        gather_steps(k)
    collect(ST2, z_from, T20)
    ST3[dp] = merge(ST2, 8)
    spread(ST3, dp, [(j, seq) for j in dp_peers], T30)

    @pl.loop(mids[2], mids[3])
    def _(k):
        gather_steps(k)
    collect(ST3, dp_from, T30)
    stat = merge(ST3, 8)
    top, ssum, esum, tsum = [stat[i:i + 1, :] for i in range(4)]
    share = ROWS[1:2, :]
    valid = ROWS[3:4, :] > 0.5
    loss = jnp.sum(jnp.where(valid, jnp.log(ssum) - tsum, 0.0), axis=1, keepdims=True) / count
    size = jnp.abs(top)
    peak = (1.0 + size) * jnp.exp(top) / ssum
    odd = jnp.where(jnp.logical_and(valid, jnp.logical_or(size > 40.0, peak > 0.25)), 1.0, 0.0)
    odd = jnp.maximum(jnp.max(odd, axis=1, keepdims=True), jnp.where(count > CAP + 0.5, 1.0, 0.0))
    scal[...] = loss
    flag[...] = odd.astype(jnp.int32)
    ROWS[4:5, :] = share / ssum
    ROWS[5:6, :] = (esum / ssum - tsum) * share * (1.0 / D)

    @pl.loop(0, VP // G)
    def _(i):
        for q in range(CH * G // VP):
            g1(i * (CH * G // VP) + q, 1).wait_recv()
        rows = rows_at(i * G, G)
        local = i * G + lax.broadcasted_iota(jnp.int32, (G, CAP), 0)
        hit = local == ROWS[2:3, :].astype(jnp.int32)
        dl = PR[rows, :].astype(F32) * ROWS[4:5, :] - jnp.where(hit, ROWS[1:2, :], 0.0)
        dlo[rows, :] = dl.astype(BF16)
        DN[...] += jnp.dot(WT[i], dlo[rows, :], preferred_element_type=F32)

    dc = rcopy(DN.at[rows_at((1 - co) * 256, 256), :], RC, DC0, core_dev)
    dc.start()
    dc.wait_recv()
    T1[...] = DN[rows_at(co * 256, 256), :] + RC[...]
    far = (4, 3, 5, 2, 6, 1, 7, 0)
    dx = []
    for n, k in enumerate(far):
        zz = lax.rem(z + k, 8)
        B1[zz] = T1[rows_at((1 - xl) * 128 + zz * 16, 16), :].astype(BF16)
        c = rcopy(B1.at[zz], RX.at[zz], DX0 + n, xlo_dev)
        c.start()
        dx.append(c)
    dz = []
    for n, k in enumerate(far):
        zz = lax.rem(z + k, 8)
        dx[n].wait_recv()
        part = T1[rows_at(xl * 128 + zz * 16, 16), :] + RX[zz].astype(F32)
        if k:
            B2[zz] = part.astype(BF16)
            c = rcopy(B2.at[zz], RZ.at[z], DZ0 + k, (dp, seq_of(zz, xl, co)))
            c.start()
            dz.append(c)
    dn = part
    for k in (1, 7, 2, 6, 3, 5, 4):
        rcopy(RZ.at[z_from[k - 1]], RZ.at[z_from[k - 1]], DZ0 + k, (dp, seq)).wait_recv()
        dn = dn + RZ[z_from[k - 1]].astype(F32)

    off = co * 256 + xl * 128 + z * 16
    rinv_row = ROWS[0:1, :]
    xn = HCT[rows_at(off, 16), :] * rinv_row
    gc = GCOL[rows_at(off, 16), 0:1]
    grow = (rinv_row * (dn * gc - xn * ROWS[5:6, :])).astype(BF16)
    ggc = jnp.sum(dn * xn, axis=1, keepdims=True)
    wide_rows = jnp.dot(grow, S[...], preferred_element_type=F32).astype(BF16)
    ghi = ggc.astype(BF16).astype(F32)
    gmid = (ggc - ghi).astype(BF16).astype(F32)
    glo = (ggc - ghi) - gmid
    lane = lax.broadcasted_iota(jnp.int32, (16, B), 1)
    gparts = jnp.where(lane == 0, ghi, jnp.where(lane == 1, gmid, jnp.where(lane == 2, glo, 0.0))).astype(BF16)
    for j in range(8):
        MB[j, 0:16, :] = wide_rows[:, j * B:(j + 1) * B]
        MB[j, 16:32, :] = gparts
    dpc = []
    for k in range(1, 8):
        c = rcopy(MB.at[dp_peers[k - 1]], RB.at[dp], DP0 + k, (dp_peers[k - 1], seq))
        c.start()
        dpc.append(c)
    RB[dp] = MB[dp]
    for k in range(1, 8):
        rcopy(RB.at[dp_from[k - 1]], RB.at[dp_from[k - 1]], DP0 + k, (dp, seq)).wait_recv()

    mine = co * 16 + xl * 8 + z
    GTX[mine, 0:B, :] = RB[:, 0:16, :].reshape(B, B)
    GTX[mine, B:B + 16, :] = jnp.transpose(RB[:, 16:32, :].reshape(B, B).astype(F32))[0:16, :].astype(BF16)

    def slice_copy(i, n, sem, dev):
        return rcopy(GTX.at[pl.ds(i, n)], GTX.at[pl.ds(i, n)], sem, dev)

    for k in (4, 3, 5, 2, 6, 1, 7):
        c = slice_copy(mine, 1, AZ0 + k, (dp, seq_of(z_peers[k - 1], xl, co)))
        c.start()
        sends.append(c)
    c = slice_copy(mine, 1, AX0, xlo_dev)
    c.start()
    sends.append(c)
    for k in (1, 7, 2, 6, 3, 5, 4):
        src = co * 16 + xl * 8 + z_from[k - 1]
        slice_copy(src, 1, AZ0 + k, (dp, seq)).wait_recv()
        c = slice_copy(src, 1, AX0 + k, xlo_dev)
        c.start()
        sends.append(c)
    c = slice_copy(co * 16 + xl * 8, 8, AC0, core_dev)
    c.start()
    sends.append(c)
    for k in (0, 1, 7, 2, 6, 3, 5, 4):
        src = co * 16 + (1 - xl) * 8 + (z_from[k - 1] if k else z)
        slice_copy(src, 1, AX0 + k, (dp, seq)).wait_recv()
    c = slice_copy(co * 16 + (1 - xl) * 8, 8, AC0 + 1, core_dev)
    c.start()
    sends.append(c)
    slice_copy((1 - co) * 16 + xl * 8, 8, AC0, core_dev).wait_recv()
    slice_copy((1 - co) * 16 + (1 - xl) * 8, 8, AC0 + 1, core_dev).wait_recv()

    for c in hsend + msend + hc + sends + [dc] + dx + dz + dpc:
        c.wait_send()

    @pl.loop(0, CH)
    def _(c):
        s1(c).wait_send()
        s2(c).wait_send()
        s3(c).wait_send()
        g3(c).wait_send()
        g2(c).wait_send()
        g1(c).wait_send()


def fused(hidden, gain, head_weight, targets, loss_mask):
    vm = pl.BlockSpec(memory_space=pltpu.VMEM)
    scratch = [
        pltpu.VMEM((8, B, W), BF16),
        pltpu.VMEM((8, 8, B), F32),
        pltpu.VMEM((VP, W), BF16),
        pltpu.VMEM((VP // G, W, G), BF16),
        pltpu.VMEM((CAP, 8 * B), BF16),
        pltpu.VMEM((W, CAP), F32),
        pltpu.VMEM((W, B), F32),
        pltpu.VMEM((8, CAP), F32),
        pltpu.VMEM((VP, CAP), BF16),
        pltpu.VMEM((CH, RH, CAP), BF16),
        pltpu.VMEM((CH, RH, CAP), BF16),
        pltpu.VMEM((CH, RQ, CAP), BF16),
        pltpu.VMEM((CH, RQ, CAP), BF16),
        pltpu.VMEM((CH, RP, CAP), BF16),
        pltpu.VMEM((8, CAP), F32),
        pltpu.VMEM((4, 8, CAP), F32),
        pltpu.VMEM((8, 8, CAP), F32),
        pltpu.VMEM((8, 8, CAP), F32),
        pltpu.VMEM((VP, CAP), BF16),
        pltpu.VMEM((W, CAP), F32),
        pltpu.VMEM((256, CAP), F32),
        pltpu.VMEM((256, CAP), F32),
        pltpu.VMEM((8, 16, CAP), BF16),
        pltpu.VMEM((8, 16, CAP), BF16),
        pltpu.VMEM((8, 16, CAP), BF16),
        pltpu.VMEM((8, 16, CAP), BF16),
        pltpu.VMEM((8, 32, B), BF16),
        pltpu.VMEM((8, 32, B), BF16),
        pltpu.SemaphoreType.DMA((NSEM,)),
        pltpu.SemaphoreType.DMA((NSEM,)),
    ]
    return pl.pallas_call(
        kernel,
        out_shape=(
            jax.ShapeDtypeStruct((VP, CAP), BF16),
            jax.ShapeDtypeStruct((CAP, W), BF16),
            jax.ShapeDtypeStruct((32, B + 16, B), BF16),
            jax.ShapeDtypeStruct((1, 1), F32),
            jax.ShapeDtypeStruct((1, 1), jnp.int32),
        ),
        in_specs=[vm] * 5,
        out_specs=(vm,) * 5,
        scratch_shapes=scratch,
        compiler_params=pltpu.CompilerParams(
            collective_id=0, has_side_effects=True, vmem_limit_bytes=44 * 1024 * 1024),
        cost_estimate=pl.CostEstimate(flops=6 * V * CAP * W, bytes_accessed=16 * 1024 * 1024, transcendentals=0),
        name="fused",
    )(hidden, gain.reshape(32, B), head_weight, targets.reshape(1, B), loss_mask.reshape(1, B))


STEPS = 8


def finish_kernel(dl, c, gtx, scal, gh, ghid, gg, loss):
    i = pl.program_id(0)
    n = VP // STEPS
    gh[...] = jnp.dot(dl[pl.ds(pl.multiple_of(i * n, 16), n), :], c[...], preferred_element_type=F32)
    block = gtx[:, pl.ds(pl.multiple_of(i * 16, 16), 16), :].reshape(W, B)
    ghid[...] = jnp.transpose(block)

    @pl.when(i == 0)
    def _():
        loss[...] = scal[...]
        parts = gtx[:, B:B + 16, :].astype(F32)
        sums = parts[:, 0, :] + parts[:, 1, :] + parts[:, 2, :]
        cols = jnp.transpose(jnp.concatenate([sums, jnp.zeros((B - 32, B), F32)], axis=0))
        row = lax.broadcasted_iota(jnp.int32, (B, B), 0)
        lane = lax.broadcasted_iota(jnp.int32, (B, B), 1)
        for q in range(4):
            pick = (row == q * 8 + lane // 16).astype(F32)
            spread = jnp.dot(cols, pick, precision=lax.Precision.HIGHEST, preferred_element_type=F32)
            spread = jnp.where(row % 16 == lane % 16, spread, 0.0)
            gg[:, q, :] = jnp.sum(spread.reshape(8, 16, B), axis=1)


def finish(dl, c, gtx, scal):
    vm = pl.BlockSpec(memory_space=pltpu.VMEM)
    n = VP // STEPS
    gh, ghid, gg, loss = pl.pallas_call(
        finish_kernel,
        grid=(STEPS,),
        out_shape=(
            jax.ShapeDtypeStruct((V, W), F32),
            jax.ShapeDtypeStruct((B, D), BF16),
            jax.ShapeDtypeStruct((8, 4, B), F32),
            jax.ShapeDtypeStruct((1, 1), F32),
        ),
        in_specs=[vm] * 4,
        out_specs=(
            pl.BlockSpec((n, W), lambda i: (i, 0)),
            pl.BlockSpec((B, W), lambda i: (0, i)),
            pl.BlockSpec((8, 4, B), lambda i: (0, 0, 0)),
            pl.BlockSpec((1, 1), lambda i: (0, 0)),
        ),
        compiler_params=pltpu.CompilerParams(vmem_limit_bytes=40 * 1024 * 1024),
        cost_estimate=pl.CostEstimate(flops=2 * V * CAP * W, bytes_accessed=8 * 1024 * 1024, transcendentals=0),
        name="finish",
    )(dl, c, gtx, scal)
    return loss.reshape(()), ghid, gg.reshape(D), gh


def norm_back(grad_normed, unit_rows, inv_rms, gain):
    grad_unit = grad_normed * gain
    return inv_rms * (
        grad_unit - unit_rows * jnp.mean(grad_unit * unit_rows, axis=-1, keepdims=True)
    )


def general(hidden, gain, head_weight, targets, loss_mask):
    floats = hidden.astype(jnp.float32)
    inv_rms = lax.rsqrt(jnp.mean(floats * floats, axis=-1, keepdims=True) + EPS)
    unit_rows = floats * inv_rms
    normed = (unit_rows * gain).astype(jnp.bfloat16)
    mask_float = loss_mask.astype(jnp.float32)
    num_valid = lax.psum(jnp.sum(mask_float), "dp")
    slices = lax.all_to_all(normed, "dp", split_axis=1, concat_axis=0, tiled=True)
    vocab_rows = head_weight.shape[0]
    logits = lax.psum_scatter(
        lax.dot_general(slices, head_weight, NT, preferred_element_type=jnp.float32),
        "dp",
        scatter_dimension=0,
        tiled=True,
    )
    column = lax.axis_index("seq") * vocab_rows + jnp.arange(vocab_rows, dtype=jnp.int32)
    one_hot = (column[None, :] == targets[:, None]).astype(jnp.float32)
    local_picked = jnp.sum(one_hot * logits, axis=1)
    row_top = lax.pmax(jnp.max(logits, axis=1), "seq")
    shifted = jnp.exp(logits - row_top[:, None])
    row_total, picked = lax.psum((jnp.sum(shifted, axis=1), local_picked), "seq")
    log_total = row_top + jnp.log(row_total)
    probs = shifted / row_total[:, None]
    row_loss = log_total - picked
    loss_value = lax.psum(jnp.sum(mask_float * row_loss), "dp") / num_valid
    dlogits = ((probs - one_hot) * (mask_float / num_valid)[:, None]).astype(jnp.bfloat16)
    shard_rows = lax.all_gather(dlogits, "dp", axis=0, tiled=True)
    grad_slices = jnp.dot(shard_rows, head_weight, preferred_element_type=jnp.float32)
    grad_head = lax.dot_general(
        shard_rows, slices, (((0,), (0,)), ((), ())), preferred_element_type=jnp.float32
    )
    returned = lax.all_to_all(grad_slices, "dp", split_axis=0, concat_axis=1, tiled=True)
    grad_normed = lax.psum(returned, "seq")
    grad_gain = lax.psum(jnp.sum(grad_normed * unit_rows, axis=0), "dp")
    grad_hidden = norm_back(grad_normed, unit_rows, inv_rms, gain).astype(jnp.bfloat16)
    return (loss_value, grad_hidden, grad_gain, grad_head)


def body(hidden, gain, head_weight, targets, loss_mask):
    dl, c, gtx, scal, flag = fused(hidden, gain, head_weight, targets, loss_mask)

    def fast(*args):
        return finish(dl, c, gtx, scal)

    return lax.cond(flag[0, 0] > 0, general, fast, hidden, gain, head_weight, targets, loss_mask)


def solution(mesh):
    return jax.shard_map(
        body,
        mesh=mesh,
        in_specs=(P("dp", None), P(), P("seq", "dp"), P("dp"), P("dp")),
        out_specs=(P(), P("dp", None), P(), P("seq", "dp")),
        check_vma=False,
    )
```

time: 740 us -> 851 us (1.15)
  Pallas kernels: 0 us -> 122 us
    pallas_call x0 -> x1, Pallas kernels: none -> 122 us  [fused(): pl.pallas_call(kernel, out_shape=(jax.ShapeDtypeStruct((VP, CAP), BF16),...]
where the time goes in v2:
time: 851 us; the launch traced here: 850 us
  waiting for transfers between devices  446 us (52%)
  blocking collectives  227 us (27%)
  Pallas kernels  122 us (14%)
  matrix products  21.1 us (2%)
  between operations  14.5 us (2%)
  other arithmetic  11.9 us (1%)
    psum x1, waiting for transfers between devices, general(): grad_normed = lax.psum(returned, 'seq')  220 us
    reduce_scatter x1, waiting for transfers between devices, general(): lax.psum_scatter(lax.dot_general(slices, head_weight, NT, preferred_eleme...  142 us
    pallas_call x1, Pallas kernels, fused(): pl.pallas_call(kernel, out_shape=(jax.ShapeDtypeStruct((VP, CAP), BF16),...  122 us
    all_gather x1, waiting for transfers between devices, general(): shard_rows = lax.all_gather(dlogits, 'dp', axis=0, tiled=True)  84.8 us
    pmax x1, blocking collectives, general(): row_top = lax.pmax(jnp.max(logits, axis=1), 'seq')  55.2 us
    psum x1, blocking collectives, general(): lax.psum((jnp.sum(shifted, axis=1), local_picked), 'seq')  53 us
    psum x1, blocking collectives, general(): loss_value = lax.psum(jnp.sum(mask_float * row_loss), 'dp') / num_valid  43 us
    all_to_all x1, blocking collectives, general(): lax.all_to_all(grad_slices, 'dp', split_axis=0, concat_axis=1, tiled=True)  30.8 us
  transfers between devices with their start and end apart: 3, of which 3 were waited for; matrix products, arithmetic and copies ran while one was open for 1% of the time, Pallas kernels for 0%

profile of v2, /device:TPU:0, one launch (start us, length us, event | category | flops | bytes accessed | tf_op | source)
XLA Modules:
  0.0 850.1 jit_solution(17445356775581316176)
XLA Ops:
  7.2 0.0 copy-start.2
  7.2 0.0 copy-start.5
  7.2 0.0 copy-start.6
  7.2 0.0 copy-start.7
  7.2 121.6 %fused.1 = (bf16[2688,640]{1,0:T(8,128)(2,1)S(1)}, bf16[640,512]{1,0:T(8,128)(2,1)S(1)}, bf16[32,144,128]{2,1,0:T(8,128)(2,1)S(1)}, f32[1,1]{1,0:T(1,128)}, s32[1,1]{1,0:T(1,128)}) custom-call(bf16[128,4096]{1,0:T(8,128)(2,1)} %hid.1, f32[32,128]{1,0:T(8,128)} %bitcast.25, bf16[2632,512]{1,0:T(8,128)(2,1)} %wgt.1, s32[1,128]{1,0:T(1,128)} %bitcast.26, ...), custom_call_target="tpu_custom_call" | custom-call | flops 5174722560 | bytes 16777216 | tf_op jit(solution)/shard_map/fused/pallas_call | solution.py:465
  129.5 0.0 copy-done.2
  129.5 0.0 copy-done.5
  129.5 0.0 copy-done.6
  129.5 0.0 copy-done.7
  129.5 713.1 %conditional.1 = (f32[2632,512]{1,0:T(8,128)}, f32[]{:T(128)}, f32[4096]{0:T(1024)}, bf16[128,4096]{1,0:T(8,128)(2,1)S(1)}) conditional(s32[]{:T(128)} %bitcast.11, (bf16[2688,640]{1,0:T(8,128)(2,1)S(1)}, bf16[640,512]{1,0:T(8,128)(2,1)S(1)}, bf16[32,144,128]{2,1,0:T(8,128)(2,1)S(1)}, f32[1,1]{1,0:T(1,128)}) %tuple.15, (s32[128]{0:T(128)S(1)}, ...), branch_computations={%region_0.0_spmd, %region_1.0_spmd} | conditional | flops 8295473664 | bytes 157989536 | solution.py:586
  129.6 0.0 reduce-scatter.2.cloned.1.call-start
  129.6 0.7 copy.18
  130.3 0.6 fusion.10
  130.9 0.7 fusion.4
  131.6 22.8 %all_to_all.30 = bf16[128,8,512]{0,2,1:T(8,128)(2,1)S(1)} all-to-all(bf16[128,8,512]{0,2,1:T(8,128)(2,1)S(1)} %bitcast.20), channel_id=1, replica_groups=mesh['dp'=8,'seq'=32] {'dp'}, dimensions={1} | all-to-all | bytes 2097152 | tf_op jit(solution)/shard_map/cond/branch_1_fun/all_to_all | solution.py:549
  154.4 0.5 copy.16
  154.9 0.0 copy-start.3
  155.0 7.9 fusion.16
  162.8 0.0 copy-done.3
  162.8 0.0 reduce-scatter.2.cloned.1.call-update
  162.8 0.0 all-gather.2.cloned.1.call-start
  162.9 141.8 %reduce-scatter.2.cloned.1.call-done = f32[128,2632]{0,1:T(8,128)} async-done(((f32[1024,2632]{0,1:T(8,128)}), f32[128,2632]{0,1:T(8,128)}) %reduce-scatter.2.cloned.1.call-update) | async-done | bytes 1347600 | tf_op jit(solution)/shard_map/cond/branch_1_fun/reduce_scatter | solution.py:551
  304.7 0.0 copy-start
  304.7 1.8 reduce_max.8
  306.5 55.2 %pmax.6 = f32[128]{0:T(128)S(1)} all-reduce(f32[128]{0:T(128)S(1)} %reduce_max.8), channel_id=1, replica_groups=mesh['dp'=8,'seq'=32] {'seq'}, use_global_device_ids=true, to_apply=%region_5.0 | all-reduce | flops 128 | bytes 1024 | tf_op jit(solution)/shard_map/cond/branch_1_fun/pmax | solution.py:560
  361.7 2.3 fusion.11
  364.0 53.0 %all-reduce = (f32[128]{0:T(128)S(1)}, f32[128]{0:T(128)S(1)}) all-reduce(f32[128]{0:T(128)S(1)} %get-tuple-element.63, f32[128]{0:T(128)S(1)} %get-tuple-element.64), channel_id=1, replica_groups=mesh['dp'=8,'seq'=32] {'seq'}, use_global_device_ids=true, to_apply=%region_9.0 | all-reduce | flops 256 | bytes 2048 | tf_op jit(solution)/shard_map/cond/branch_1_fun/psum | solution.py:562
  417.0 0.6 multiply_reduce_fusion
  417.6 22.1 %psum.39 = f32[]{:T(128)} all-reduce(f32[]{:T(128)} %get-tuple-element.66), channel_id=1, replica_groups=mesh['dp'=8,'seq'=32] {'dp'}, use_global_device_ids=true, to_apply=%region_13.0 | all-reduce | flops 1 | bytes 8 | tf_op jit(solution)/shard_map/cond/branch_1_fun/psum | solution.py:548
  439.7 0.6 convert_divide_fusion
  440.3 0.0 copy-done
  440.3 2.0 fusion.14
  442.3 0.0 all-gather.2.cloned.1.call-update
  442.3 0.2 all-reduce.4.cloned.1.call-start
  442.5 84.8 %all-gather.2.cloned.1.call-done = bf16[1024,2632]{0,1:T(8,128)(2,1)} async-done(((bf16[128,2632]{0,1:T(8,128)(2,1)}), bf16[1024,2632]{0,1:T(8,128)(2,1)}) %all-gather.2.cloned.1.call-update) | async-done | bytes 5390352 | tf_op jit(solution)/shard_map/cond/branch_1_fun/all_gather | solution.py:568
  527.3 6.0 fusion.17
  533.2 30.8 %all_to_all.31 = f32[8,128,512]{2,1,0:T(8,128)S(1)} all-to-all(f32[8,128,512]{2,1,0:T(8,128)S(1)} %bitcast.22), channel_id=1, replica_groups=mesh['dp'=8,'seq'=32] {'dp'}, dimensions={0} | all-to-all | bytes 4194304 | tf_op jit(solution)/shard_map/cond/branch_1_fun/all_to_all | solution.py:573
  564.0 1.9 copy.17
  565.9 0.0 all-reduce.4.cloned.1.call-update
  565.9 1.2 copy-done.4
  567.1 7.2 fusion.18
  574.4 219.5 %all-reduce.4.cloned.1.call-done = f32[128,4096]{0,1:T(8,128)} async-done(((f32[128,4096]{0,1:T(8,128)}), f32[128,4096]{0,1:T(8,128)}) %all-reduce.4.cloned.1.call-update) | async-done | bytes 2097168 | tf_op jit(solution)/shard_map/cond/branch_1_fun/psum | solution.py:574
  793.9 2.6 fusion.5
  796.6 0.0 copy-done.1
  796.6 0.7 fusion.8
  797.3 0.5 copy.21
  797.9 43.0 %all-reduce.1 = (f32[]{:T(128)}, f32[4096]{0:T(1024)}) all-reduce(f32[]{:T(128)} %get-tuple-element.65, f32[4096]{0:T(1024)S(1)} %get-tuple-element.62), channel_id=1, replica_groups=mesh['dp'=8,'seq'=32] {'dp'}, use_global_device_ids=true, to_apply=%region_11.0 | all-reduce | flops 4097 | bytes 32776 | tf_op jit(solution)/shard_map/cond/branch_1_fun/psum | solution.py:566
  842.6 1.0 copy-done.8
  (6 shorter events, 0.0 us)
Async XLA Ops:
  7.2 122.3 %copy-start.2 = (bf16[128,4096]{1,0:T(8,128)(2,1)S(1)}, bf16[128,4096]{1,0:T(8,128)(2,1)}, u32[]{:S(2)}) copy-start(bf16[128,4096]{1,0:T(8,128)(2,1)} %hid.1) | copy-start | bytes 3145732
  7.2 122.3 %copy-start.5 = (f32[4096]{0:T(1024)S(1)}, f32[4096]{0:T(1024)}, u32[]{:S(2)}) copy-start(f32[4096]{0:T(1024)} %param.8) | copy-start | bytes 49156
  7.2 122.3 %copy-start.6 = (s32[128]{0:T(128)S(1)}, s32[128]{0:T(128)}, u32[]{:S(2)}) copy-start(s32[128]{0:T(128)} %param.10) | copy-start | bytes 1540
  7.2 122.3 %copy-start.7 = (s32[128]{0:T(128)S(1)}, s32[128]{0:T(128)}, u32[]{:S(2)}) copy-start(s32[128]{0:T(128)} %param.11) | copy-start | bytes 1540
  129.6 175.1 %reduce-scatter.2.cloned.1.call-start = ((), (), s32[]{:S(2)}) async-start(), calls=%async_computation.3 | async-start | bytes 12128256 | tf_op jit(solution)/shard_map/cond/branch_1_fun/reduce_scatter | solution.py:551
  154.9 7.9 copy-start.3
  162.8 364.4 %all-gather.2.cloned.1.call-start = ((), (), s32[]{:S(2)}) async-start(), calls=%async_computation.4 | async-start | bytes 6064128 | tf_op jit(solution)/shard_map/cond/branch_1_fun/all_gather | solution.py:568
  304.7 135.6 %copy-start = (f32[128,2632]{0,1:T(8,128)S(1)}, f32[128,2632]{0,1:T(8,128)}, u32[]{:S(2)}) copy-start(f32[128,2632]{0,1:T(8,128)} %reduce-scatter.2.cloned.1.call-done) | copy-start | bytes 4042756 | tf_op jit(solution)/shard_map/cond
  442.3 351.6 %all-reduce.4.cloned.1.call-start = ((), (), s32[]{:S(2)}) async-start(), calls=%async_computation.5 | async-start | bytes 4194304 | tf_op jit(solution)/shard_map/cond/branch_1_fun/psum | solution.py:574
  565.9 1.2 copy-start.4
  793.9 2.7 copy-start.1
  842.6 1.0 copy-start.8
Sparse Core Ops, SparseCore 0:
  163.0 141.6 reduce-scatter.1
  442.4 84.8 all-gather.1
  566.0 227.8 all-reduce.3

commit v3 on v2

--- a/solution.py
+++ b/solution.py
@@ -17,13 +17,13 @@
 V = 2632
 VP = 2688
 CAP = 640
-CH = 7
+CH = 21
 R = VP // CH
 RH, RQ, RP = R // 2, R // 4, R // 8
 G = 384
 LOW = -1e30
 
-LAG1, LAG2, LAG3, LAG4, LAG5 = 2, 3, 4, 6, 8
+LAG1, LAG2, LAG3, LAG4, LAG5 = 8, 14, 20, 28, 36
 
 NSEM = 0
 
@@ -37,12 +37,12 @@
 H0, M0, HC0 = sems(8), sems(8), sems(8)
 S10, S20, S30, G30, G20, G10 = [sems(CH) for _ in range(6)]
 T10, T20, T30 = sems(4), sems(8), sems(8)
-DC0, DX0, DZ0, DP0, AZ0, AX0, AC0 = sems(1), sems(8), sems(8), sems(8), sems(8), sems(8), sems(2)
-
-
-def kernel(hid, gain, wgt, tgt, msk, dlo, C, GTX, scal, flag,
-           H, META, WP, WT, S, HCT, GCOL, ROWS, L, R1, A1, R2, A2, R3, STAT, ST1, ST2, ST3,
-           PR, DN, RC, T1, B1, RX, B2, RZ, MB, RB, ss, rs):
+DC0, DX0, DZ0, DP0, AZ0, AX0, AC0 = sems(1), sems(8), sems(8), sems(8), sems(8), sems(8), sems(16)
+
+
+def kernel(hid_in, gain, wgt_in, tgt, msk, dlo, C, ghid, gg, scal, flag,
+           hid, wgt, GTX, H, META, WP, WT, S, HCT, GCOL, ROWS, L, R1, A1, R2, A2, R3, STAT, ST1, ST2, ST3,
+           PR, DN, RC, T1, B1, RX, B2, RZ, MB, RB, ss, rs, ls):
     dp = lax.axis_index("dp")
     seq = lax.axis_index("seq")
     y, xh = dp // 2, dp % 2
@@ -72,6 +72,11 @@
     core_dev = (dp, seq_of(z, xl, 1 - co))
     xlo_dev = (dp, seq_of(z, 1 - xl, co))
 
+    fetch_hid = pltpu.make_async_copy(hid_in, hid, ls.at[0])
+    fetch_hid.start()
+    fetch_wgt = pltpu.make_async_copy(wgt_in, wgt, ls.at[1])
+    fetch_wgt.start()
+
     barrier = pltpu.get_barrier_semaphore()
     for j in dp_peers:
         pl.semaphore_signal(barrier, inc=1, device_id=(j, seq), device_id_type=MESH)
@@ -80,6 +85,7 @@
     for zz in z_peers:
         pl.semaphore_signal(barrier, inc=1, device_id=(dp, seq_of(zz, xl, co)), device_id_type=MESH)
 
+    fetch_hid.wait()
     total = jnp.zeros((B, 1), F32)
     for j in range(8):
         x = hid[:, j * W:(j + 1) * W].astype(F32)
@@ -104,6 +110,7 @@
         c.start()
         hsend.append(c)
 
+    fetch_wgt.wait()
     for i in range(6):
         WP[i * G:(i + 1) * G, :] = wgt[i * G:(i + 1) * G, :]
     WP[6 * G:V - 8, :] = wgt[6 * G:V - 8, :]
@@ -387,33 +394,56 @@
     GTX[mine, 0:B, :] = RB[:, 0:16, :].reshape(B, B)
     GTX[mine, B:B + 16, :] = jnp.transpose(RB[:, 16:32, :].reshape(B, B).astype(F32))[0:16, :].astype(BF16)
 
-    def slice_copy(i, n, sem, dev):
-        return rcopy(GTX.at[pl.ds(i, n)], GTX.at[pl.ds(i, n)], sem, dev)
-
-    for k in (4, 3, 5, 2, 6, 1, 7):
-        c = slice_copy(mine, 1, AZ0 + k, (dp, seq_of(z_peers[k - 1], xl, co)))
+    def slice_copy(i, sem, dev):
+        return rcopy(GTX.at[i], GTX.at[i], sem, dev)
+
+    def forward(i, sem, dev):
+        c = slice_copy(i, sem, dev)
         c.start()
         sends.append(c)
-    c = slice_copy(mine, 1, AX0, xlo_dev)
-    c.start()
-    sends.append(c)
-    for k in (1, 7, 2, 6, 3, 5, 4):
+
+    row = lax.broadcasted_iota(jnp.int32, (B, B), 0)
+    lane = lax.broadcasted_iota(jnp.int32, (B, B), 1)
+    pick = (row == lane // 16).astype(F32)
+    diag = row % 16 == lane % 16
+
+    def emit(cc, xx):
+        q = cc * 2 + xx
+        at = pl.ds(q * 8, 8)
+        for j in range(8):
+            block = GTX[at, j * 16:(j + 1) * 16, :].reshape(B, B)
+            ghid[:, pl.ds(pl.multiple_of(j * W + q * B, B), B)] = jnp.transpose(block)
+        parts = GTX[at, B:B + 16, :].astype(F32)
+        sums = parts[:, 0, :] + parts[:, 1, :] + parts[:, 2, :]
+        cols = jnp.transpose(jnp.concatenate([sums, jnp.zeros((B - 8, B), F32)], axis=0))
+        spread = jnp.dot(cols, pick, precision=lax.Precision.HIGHEST, preferred_element_type=F32)
+        spread = jnp.sum(jnp.where(diag, spread, 0.0).reshape(8, 16, B), axis=1)
+        for j in range(8):
+            gg[pl.ds(j * 4 + q, 1), :] = spread[j:j + 1, :]
+
+    near = (1, 7, 2, 6, 3, 5, 4)
+    ox, oc = 1 - xl, 1 - co
+    for k in (4, 3, 5, 2, 6, 1, 7):
+        forward(mine, AZ0 + k, (dp, seq_of(z_peers[k - 1], xl, co)))
+    forward(mine, AX0, xlo_dev)
+    forward(mine, AC0, core_dev)
+    for k in near:
         src = co * 16 + xl * 8 + z_from[k - 1]
-        slice_copy(src, 1, AZ0 + k, (dp, seq)).wait_recv()
-        c = slice_copy(src, 1, AX0 + k, xlo_dev)
-        c.start()
-        sends.append(c)
-    c = slice_copy(co * 16 + xl * 8, 8, AC0, core_dev)
-    c.start()
-    sends.append(c)
-    for k in (0, 1, 7, 2, 6, 3, 5, 4):
-        src = co * 16 + (1 - xl) * 8 + (z_from[k - 1] if k else z)
-        slice_copy(src, 1, AX0 + k, (dp, seq)).wait_recv()
-    c = slice_copy(co * 16 + (1 - xl) * 8, 8, AC0 + 1, core_dev)
-    c.start()
-    sends.append(c)
-    slice_copy((1 - co) * 16 + xl * 8, 8, AC0, core_dev).wait_recv()
-    slice_copy((1 - co) * 16 + (1 - xl) * 8, 8, AC0 + 1, core_dev).wait_recv()
+        slice_copy(src, AZ0 + k, (dp, seq)).wait_recv()
+        forward(src, AX0 + k, xlo_dev)
+        forward(src, AC0 + k, core_dev)
+    emit(co, xl)
+    for k in (0,) + near:
+        src = co * 16 + ox * 8 + (z_from[k - 1] if k else z)
+        slice_copy(src, AX0 + k, (dp, seq)).wait_recv()
+        forward(src, AC0 + 8 + k, core_dev)
+    emit(co, ox)
+    for k in (0,) + near:
+        slice_copy(oc * 16 + xl * 8 + (z_from[k - 1] if k else z), AC0 + k, (dp, seq)).wait_recv()
+    emit(oc, xl)
+    for k in (0,) + near:
+        slice_copy(oc * 16 + ox * 8 + (z_from[k - 1] if k else z), AC0 + 8 + k, (dp, seq)).wait_recv()
+    emit(oc, ox)
 
     for c in hsend + msend + hc + sends + [dc] + dx + dz + dpc:
         c.wait_send()
@@ -430,7 +460,11 @@
 
 def fused(hidden, gain, head_weight, targets, loss_mask):
     vm = pl.BlockSpec(memory_space=pltpu.VMEM)
+    hbm = pl.BlockSpec(memory_space=pl.ANY)
     scratch = [
+        pltpu.VMEM((B, D), BF16),
+        pltpu.VMEM((V, W), BF16),
+        pltpu.VMEM((32, B + 16, B), BF16),
         pltpu.VMEM((8, B, W), BF16),
         pltpu.VMEM((8, 8, B), F32),
         pltpu.VMEM((VP, W), BF16),
@@ -461,18 +495,20 @@
         pltpu.VMEM((8, 32, B), BF16),
         pltpu.SemaphoreType.DMA((NSEM,)),
         pltpu.SemaphoreType.DMA((NSEM,)),
+        pltpu.SemaphoreType.DMA((2,)),
     ]
     return pl.pallas_call(
         kernel,
         out_shape=(
             jax.ShapeDtypeStruct((VP, CAP), BF16),
             jax.ShapeDtypeStruct((CAP, W), BF16),
-            jax.ShapeDtypeStruct((32, B + 16, B), BF16),
+            jax.ShapeDtypeStruct((B, D), BF16),
+            jax.ShapeDtypeStruct((32, B), F32),
             jax.ShapeDtypeStruct((1, 1), F32),
             jax.ShapeDtypeStruct((1, 1), jnp.int32),
         ),
-        in_specs=[vm] * 5,
-        out_specs=(vm,) * 5,
+        in_specs=[hbm, vm, hbm, vm, vm],
+        out_specs=(vm,) * 6,
         scratch_shapes=scratch,
         compiler_params=pltpu.CompilerParams(
             collective_id=0, has_side_effects=True, vmem_limit_bytes=44 * 1024 * 1024),
@@ -484,52 +520,48 @@
 STEPS = 8
 
 
-def finish_kernel(dl, c, gtx, scal, gh, ghid, gg, loss):
+def finish_kernel(dl, c, ghid, gg, scal, gh, ghid_out, gg_out, loss, fs):
     i = pl.program_id(0)
     n = VP // STEPS
-    gh[...] = jnp.dot(dl[pl.ds(pl.multiple_of(i * n, 16), n), :], c[...], preferred_element_type=F32)
-    block = gtx[:, pl.ds(pl.multiple_of(i * 16, 16), 16), :].reshape(W, B)
-    ghid[...] = jnp.transpose(block)
+    rows = pltpu.make_async_copy(ghid, ghid_out, fs.at[0])
 
     @pl.when(i == 0)
     def _():
+        rows.start()
+        gg_out[...] = gg[...]
         loss[...] = scal[...]
-        parts = gtx[:, B:B + 16, :].astype(F32)
-        sums = parts[:, 0, :] + parts[:, 1, :] + parts[:, 2, :]
-        cols = jnp.transpose(jnp.concatenate([sums, jnp.zeros((B - 32, B), F32)], axis=0))
-        row = lax.broadcasted_iota(jnp.int32, (B, B), 0)
-        lane = lax.broadcasted_iota(jnp.int32, (B, B), 1)
-        for q in range(4):
-            pick = (row == q * 8 + lane // 16).astype(F32)
-            spread = jnp.dot(cols, pick, precision=lax.Precision.HIGHEST, preferred_element_type=F32)
-            spread = jnp.where(row % 16 == lane % 16, spread, 0.0)
-            gg[:, q, :] = jnp.sum(spread.reshape(8, 16, B), axis=1)
-
-
-def finish(dl, c, gtx, scal):
+
+    gh[...] = jnp.dot(dl[pl.ds(pl.multiple_of(i * n, 16), n), :], c[...], preferred_element_type=F32)
+
+    @pl.when(i == STEPS - 1)
+    def _():
+        rows.wait()
+
+
+def finish(dl, c, ghid, gg, scal):
     vm = pl.BlockSpec(memory_space=pltpu.VMEM)
     n = VP // STEPS
-    gh, ghid, gg, loss = pl.pallas_call(
+    return pl.pallas_call(
         finish_kernel,
         grid=(STEPS,),
         out_shape=(
             jax.ShapeDtypeStruct((V, W), F32),
             jax.ShapeDtypeStruct((B, D), BF16),
-            jax.ShapeDtypeStruct((8, 4, B), F32),
+            jax.ShapeDtypeStruct((32, B), F32),
             jax.ShapeDtypeStruct((1, 1), F32),
         ),
-        in_specs=[vm] * 4,
+        in_specs=[vm] * 5,
         out_specs=(
             pl.BlockSpec((n, W), lambda i: (i, 0)),
-            pl.BlockSpec((B, W), lambda i: (0, i)),
-            pl.BlockSpec((8, 4, B), lambda i: (0, 0, 0)),
+            pl.BlockSpec(memory_space=pltpu.HBM),
+            pl.BlockSpec((32, B), lambda i: (0, 0)),
             pl.BlockSpec((1, 1), lambda i: (0, 0)),
         ),
+        scratch_shapes=[pltpu.SemaphoreType.DMA((1,))],
         compiler_params=pltpu.CompilerParams(vmem_limit_bytes=40 * 1024 * 1024),
         cost_estimate=pl.CostEstimate(flops=2 * V * CAP * W, bytes_accessed=8 * 1024 * 1024, transcendentals=0),
         name="finish",
-    )(dl, c, gtx, scal)
-    return loss.reshape(()), ghid, gg.reshape(D), gh
+    )(dl, c, ghid, gg, scal)
 
 
 def norm_back(grad_normed, unit_rows, inv_rms, gain):
@@ -578,10 +610,11 @@
 
 
 def body(hidden, gain, head_weight, targets, loss_mask):
-    dl, c, gtx, scal, flag = fused(hidden, gain, head_weight, targets, loss_mask)
+    dl, c, ghid, gg, scal, flag = fused(hidden, gain, head_weight, targets, loss_mask)
 
     def fast(*args):
-        return finish(dl, c, gtx, scal)
+        gh, ghid_out, gg_out, loss = finish(dl, c, ghid, gg, scal)
+        return loss.reshape(()), ghid_out, gg_out.reshape(D), gh
 
     return lax.cond(flag[0, 0] > 0, general, fast, hidden, gain, head_weight, targets, loss_mask)
 

time: 851 us -> 836 us (0.982)
  Pallas kernels: 122 us -> 107 us
    pallas_call x1, Pallas kernels: 122 us -> 107 us  [fused(): pl.pallas_call(kernel, out_shape=(jax.ShapeDtypeStruct((VP, CAP), BF16),...]
where the time goes in v3:
time: 836 us; the launch traced here: 835 us
  waiting for transfers between devices  445 us (53%)
  blocking collectives  228 us (27%)
  Pallas kernels  107 us (13%)
  matrix products  21.1 us (3%)
  between operations  14.5 us (2%)
  other arithmetic  11.9 us (1%)
    psum x1, waiting for transfers between devices, general(): grad_normed = lax.psum(returned, 'seq')  219 us
    reduce_scatter x1, waiting for transfers between devices, general(): lax.psum_scatter(lax.dot_general(slices, head_weight, NT, preferred_eleme...  141 us
    pallas_call x1, Pallas kernels, fused(): pl.pallas_call(kernel, out_shape=(jax.ShapeDtypeStruct((VP, CAP), BF16),...  107 us
    all_gather x1, waiting for transfers between devices, general(): shard_rows = lax.all_gather(dlogits, 'dp', axis=0, tiled=True)  85 us
    pmax x1, blocking collectives, general(): row_top = lax.pmax(jnp.max(logits, axis=1), 'seq')  55.2 us
    psum x1, blocking collectives, general(): lax.psum((jnp.sum(shifted, axis=1), local_picked), 'seq')  53 us
    psum x1, blocking collectives, general(): loss_value = lax.psum(jnp.sum(mask_float * row_loss), 'dp') / num_valid  43 us
    all_to_all x1, blocking collectives, general(): lax.all_to_all(grad_slices, 'dp', split_axis=0, concat_axis=1, tiled=True)  30.8 us
  transfers between devices with their start and end apart: 3, of which 3 were waited for; matrix products, arithmetic and copies ran while one was open for 1% of the time, Pallas kernels for 0%

profile of v3, /device:TPU:0, one launch (start us, length us, event | category | flops | bytes accessed | tf_op | source)
XLA Modules:
  0.0 835.4 jit_solution(11691147092138219437)
XLA Ops:
  7.2 0.0 copy-start.2
  7.2 0.0 copy-start.5
  7.2 0.0 copy-start.6
  7.2 0.0 copy-start.7
  7.2 106.6 %fused.1 = (bf16[2688,640]{1,0:T(8,128)(2,1)S(1)}, bf16[640,512]{1,0:T(8,128)(2,1)S(1)}, bf16[128,4096]{1,0:T(8,128)(2,1)S(1)}, f32[32,128]{1,0:T(8,128)S(1)}, f32[1,1]{1,0:T(1,128)}, /*index=5*/s32[1,1]{1,0:T(1,128)}) custom-call(bf16[128,4096]{1,0:T(8,128)(2,1)} %hid_in.1, f32[32,128]{1,0:T(8,128)} %bitcast.25, bf16[2632,512]{1,0:T(8,128)(2,1)} %wgt_in.1, ...), custom_call_target="tpu_custom_call" | custom-call | flops 5174722560 | bytes 16777216 | tf_op jit(solution)/shard_map/fused/pallas_call | solution.py:500
  114.5 0.0 copy-done.2
  114.5 0.0 copy-done.5
  114.5 0.0 copy-done.6
  114.5 0.0 copy-done.7
  114.5 713.4 %conditional.1 = (f32[2632,512]{1,0:T(8,128)}, f32[]{:T(128)}, f32[4096]{0:T(1024)}, bf16[128,4096]{1,0:T(8,128)(2,1)S(1)}) conditional(s32[]{:T(128)} %bitcast.11, (bf16[2688,640]{1,0:T(8,128)(2,1)S(1)}, bf16[640,512]{1,0:T(8,128)(2,1)S(1)}, bf16[128,4096]{1,0:T(8,128)(2,1)S(1)}, f32[32,128]{1,0:T(8,128)S(1)}, f32[1,1]{1,0:T(1,128)}) %tuple.15, ...), branch_computations={%region_0.0_spmd, %region_1.0_spmd} | conditional | flops 8295473664 | bytes 157989536 | solution.py:619
  114.6 0.0 reduce-scatter.2.cloned.1.call-start
  114.6 0.7 copy.18
  115.3 0.6 fusion.10
  115.9 0.7 fusion.4
  116.6 23.9 %all_to_all.30 = bf16[128,8,512]{0,2,1:T(8,128)(2,1)S(1)} all-to-all(bf16[128,8,512]{0,2,1:T(8,128)(2,1)S(1)} %bitcast.20), channel_id=1, replica_groups=mesh['dp'=8,'seq'=32] {'dp'}, dimensions={1} | all-to-all | bytes 2097152 | tf_op jit(solution)/shard_map/cond/branch_1_fun/all_to_all | solution.py:581
  140.5 0.5 copy.16
  141.1 0.0 copy-start.3
  141.1 7.9 fusion.16
  148.9 0.0 copy-done.3
  148.9 0.0 reduce-scatter.2.cloned.1.call-update
  149.0 0.0 all-gather.2.cloned.1.call-start
  149.0 141.1 %reduce-scatter.2.cloned.1.call-done = f32[128,2632]{0,1:T(8,128)} async-done(((f32[1024,2632]{0,1:T(8,128)}), f32[128,2632]{0,1:T(8,128)}) %reduce-scatter.2.cloned.1.call-update) | async-done | bytes 1347600 | tf_op jit(solution)/shard_map/cond/branch_1_fun/reduce_scatter | solution.py:583
  290.1 0.0 copy-start
  290.1 1.8 reduce_max.8
  291.9 55.2 %pmax.6 = f32[128]{0:T(128)S(1)} all-reduce(f32[128]{0:T(128)S(1)} %reduce_max.8), channel_id=1, replica_groups=mesh['dp'=8,'seq'=32] {'seq'}, use_global_device_ids=true, to_apply=%region_5.0 | all-reduce | flops 128 | bytes 1024 | tf_op jit(solution)/shard_map/cond/branch_1_fun/pmax | solution.py:592
  347.0 2.3 fusion.11
  349.3 53.0 %all-reduce = (f32[128]{0:T(128)S(1)}, f32[128]{0:T(128)S(1)}) all-reduce(f32[128]{0:T(128)S(1)} %get-tuple-element.68, f32[128]{0:T(128)S(1)} %get-tuple-element.69), channel_id=1, replica_groups=mesh['dp'=8,'seq'=32] {'seq'}, use_global_device_ids=true, to_apply=%region_9.0 | all-reduce | flops 256 | bytes 2048 | tf_op jit(solution)/shard_map/cond/branch_1_fun/psum | solution.py:594
  402.3 0.6 multiply_reduce_fusion
  402.9 22.2 %psum.39 = f32[]{:T(128)} all-reduce(f32[]{:T(128)} %get-tuple-element.71), channel_id=1, replica_groups=mesh['dp'=8,'seq'=32] {'dp'}, use_global_device_ids=true, to_apply=%region_13.0 | all-reduce | flops 1 | bytes 8 | tf_op jit(solution)/shard_map/cond/branch_1_fun/psum | solution.py:580
  425.2 0.6 convert_divide_fusion
  425.8 0.0 copy-done
  425.8 2.0 fusion.14
  427.8 0.0 all-gather.2.cloned.1.call-update
  427.8 0.0 all-reduce.4.cloned.1.call-start
  427.9 85.0 %all-gather.2.cloned.1.call-done = bf16[1024,2632]{0,1:T(8,128)(2,1)} async-done(((bf16[128,2632]{0,1:T(8,128)(2,1)}), bf16[1024,2632]{0,1:T(8,128)(2,1)}) %all-gather.2.cloned.1.call-update) | async-done | bytes 5390352 | tf_op jit(solution)/shard_map/cond/branch_1_fun/all_gather | solution.py:600
  512.8 6.0 fusion.17
  518.8 30.8 %all_to_all.31 = f32[8,128,512]{2,1,0:T(8,128)S(1)} all-to-all(f32[8,128,512]{2,1,0:T(8,128)S(1)} %bitcast.22), channel_id=1, replica_groups=mesh['dp'=8,'seq'=32] {'dp'}, dimensions={0} | all-to-all | bytes 4194304 | tf_op jit(solution)/shard_map/cond/branch_1_fun/all_to_all | solution.py:605
  549.6 1.9 copy.17
  551.5 0.0 all-reduce.4.cloned.1.call-update
  551.5 1.2 copy-done.4
  552.7 7.2 fusion.18
  559.9 219.2 %all-reduce.4.cloned.1.call-done = f32[128,4096]{0,1:T(8,128)} async-done(((f32[128,4096]{0,1:T(8,128)}), f32[128,4096]{0,1:T(8,128)}) %all-reduce.4.cloned.1.call-update) | async-done | bytes 2097168 | tf_op jit(solution)/shard_map/cond/branch_1_fun/psum | solution.py:606
  779.2 2.6 fusion.5
  781.8 0.0 copy-done.1
  781.8 0.7 fusion.8
  782.6 0.5 copy.21
  783.1 43.0 %all-reduce.1 = (f32[]{:T(128)}, f32[4096]{0:T(1024)}) all-reduce(f32[]{:T(128)} %get-tuple-element.70, f32[4096]{0:T(1024)S(1)} %get-tuple-element.67), channel_id=1, replica_groups=mesh['dp'=8,'seq'=32] {'dp'}, use_global_device_ids=true, to_apply=%region_11.0 | all-reduce | flops 4097 | bytes 32776 | tf_op jit(solution)/shard_map/cond/branch_1_fun/psum | solution.py:598
  827.9 1.0 copy-done.8
  (6 shorter events, 0.0 us)
Async XLA Ops:
  7.2 107.3 %copy-start.2 = (bf16[128,4096]{1,0:T(8,128)(2,1)S(1)}, bf16[128,4096]{1,0:T(8,128)(2,1)}, u32[]{:S(2)}) copy-start(bf16[128,4096]{1,0:T(8,128)(2,1)} %hid_in.1) | copy-start | bytes 3145732
  7.2 107.3 %copy-start.5 = (f32[4096]{0:T(1024)S(1)}, f32[4096]{0:T(1024)}, u32[]{:S(2)}) copy-start(f32[4096]{0:T(1024)} %param.8) | copy-start | bytes 49156
  7.2 107.3 %copy-start.6 = (s32[128]{0:T(128)S(1)}, s32[128]{0:T(128)}, u32[]{:S(2)}) copy-start(s32[128]{0:T(128)} %param.10) | copy-start | bytes 1540
  7.2 107.3 %copy-start.7 = (s32[128]{0:T(128)S(1)}, s32[128]{0:T(128)}, u32[]{:S(2)}) copy-start(s32[128]{0:T(128)} %param.11) | copy-start | bytes 1540
  114.6 175.5 %reduce-scatter.2.cloned.1.call-start = ((), (), s32[]{:S(2)}) async-start(), calls=%async_computation.3 | async-start | bytes 12128256 | tf_op jit(solution)/shard_map/cond/branch_1_fun/reduce_scatter | solution.py:583
  141.1 7.9 copy-start.3
  149.0 363.9 %all-gather.2.cloned.1.call-start = ((), (), s32[]{:S(2)}) async-start(), calls=%async_computation.4 | async-start | bytes 6064128 | tf_op jit(solution)/shard_map/cond/branch_1_fun/all_gather | solution.py:600
  290.1 135.7 %copy-start = (f32[128,2632]{0,1:T(8,128)S(1)}, f32[128,2632]{0,1:T(8,128)}, u32[]{:S(2)}) copy-start(f32[128,2632]{0,1:T(8,128)} %reduce-scatter.2.cloned.1.call-done) | copy-start | bytes 4042756 | tf_op jit(solution)/shard_map/cond
  427.8 351.4 %all-reduce.4.cloned.1.call-start = ((), (), s32[]{:S(2)}) async-start(), calls=%async_computation.5 | async-start | bytes 4194304 | tf_op jit(solution)/shard_map/cond/branch_1_fun/psum | solution.py:606
  551.5 1.2 copy-start.4
  779.2 2.7 copy-start.1
  827.9 1.0 copy-start.8
Sparse Core Ops, SparseCore 0:
  149.1 140.9 reduce-scatter.1
  427.9 84.8 all-gather.1
  551.6 227.5 all-reduce.3

commit v4 on v3

--- a/solution.py
+++ b/solution.py
@@ -347,7 +347,7 @@
     dx = []
     for n, k in enumerate(far):
         zz = lax.rem(z + k, 8)
-        B1[zz] = T1[rows_at((1 - xl) * 128 + zz * 16, 16), :].astype(BF16)
+        B1[zz] = T1[rows_at((1 - xl) * 128 + zz * 16, 16), :]
         c = rcopy(B1.at[zz], RX.at[zz], DX0 + n, xlo_dev)
         c.start()
         dx.append(c)
@@ -355,16 +355,16 @@
     for n, k in enumerate(far):
         zz = lax.rem(z + k, 8)
         dx[n].wait_recv()
-        part = T1[rows_at(xl * 128 + zz * 16, 16), :] + RX[zz].astype(F32)
+        part = T1[rows_at(xl * 128 + zz * 16, 16), :] + RX[zz]
         if k:
-            B2[zz] = part.astype(BF16)
+            B2[zz] = part
             c = rcopy(B2.at[zz], RZ.at[z], DZ0 + k, (dp, seq_of(zz, xl, co)))
             c.start()
             dz.append(c)
     dn = part
     for k in (1, 7, 2, 6, 3, 5, 4):
         rcopy(RZ.at[z_from[k - 1]], RZ.at[z_from[k - 1]], DZ0 + k, (dp, seq)).wait_recv()
-        dn = dn + RZ[z_from[k - 1]].astype(F32)
+        dn = dn + RZ[z_from[k - 1]]
 
     off = co * 256 + xl * 128 + z * 16
     rinv_row = ROWS[0:1, :]
@@ -487,10 +487,10 @@
         pltpu.VMEM((W, CAP), F32),
         pltpu.VMEM((256, CAP), F32),
         pltpu.VMEM((256, CAP), F32),
-        pltpu.VMEM((8, 16, CAP), BF16),
-        pltpu.VMEM((8, 16, CAP), BF16),
-        pltpu.VMEM((8, 16, CAP), BF16),
-        pltpu.VMEM((8, 16, CAP), BF16),
+        pltpu.VMEM((8, 16, CAP), F32),
+        pltpu.VMEM((8, 16, CAP), F32),
+        pltpu.VMEM((8, 16, CAP), F32),
+        pltpu.VMEM((8, 16, CAP), F32),
         pltpu.VMEM((8, 32, B), BF16),
         pltpu.VMEM((8, 32, B), BF16),
         pltpu.SemaphoreType.DMA((NSEM,)),
@@ -571,40 +571,53 @@
     )
 
 
+def spread_all(x, name):
+    n = lax.axis_size(name)
+    copies = jnp.broadcast_to(x[None], (n,) + x.shape)
+    return lax.all_to_all(copies, name, split_axis=0, concat_axis=0, tiled=True)
+
+
+def scatter_sum(x, name):
+    n = lax.axis_size(name)
+    parts = lax.all_to_all(x, name, split_axis=0, concat_axis=0, tiled=True)
+    return jnp.sum(parts.reshape((n, x.shape[0] // n) + x.shape[1:]), axis=0)
+
+
+def total(x, name):
+    return jnp.sum(spread_all(x, name), axis=0)
+
+
 def general(hidden, gain, head_weight, targets, loss_mask):
     floats = hidden.astype(jnp.float32)
     inv_rms = lax.rsqrt(jnp.mean(floats * floats, axis=-1, keepdims=True) + EPS)
     unit_rows = floats * inv_rms
     normed = (unit_rows * gain).astype(jnp.bfloat16)
     mask_float = loss_mask.astype(jnp.float32)
-    num_valid = lax.psum(jnp.sum(mask_float), "dp")
+    num_valid = total(jnp.sum(mask_float).reshape(1), "dp")[0]
     slices = lax.all_to_all(normed, "dp", split_axis=1, concat_axis=0, tiled=True)
     vocab_rows = head_weight.shape[0]
-    logits = lax.psum_scatter(
-        lax.dot_general(slices, head_weight, NT, preferred_element_type=jnp.float32),
-        "dp",
-        scatter_dimension=0,
-        tiled=True,
-    )
+    logits = scatter_sum(
+        lax.dot_general(slices, head_weight, NT, preferred_element_type=jnp.float32), "dp")
     column = lax.axis_index("seq") * vocab_rows + jnp.arange(vocab_rows, dtype=jnp.int32)
     one_hot = (column[None, :] == targets[:, None]).astype(jnp.float32)
     local_picked = jnp.sum(one_hot * logits, axis=1)
-    row_top = lax.pmax(jnp.max(logits, axis=1), "seq")
+    row_top = jnp.max(spread_all(jnp.max(logits, axis=1), "seq"), axis=0)
     shifted = jnp.exp(logits - row_top[:, None])
-    row_total, picked = lax.psum((jnp.sum(shifted, axis=1), local_picked), "seq")
+    row_total, picked = total(jnp.stack([jnp.sum(shifted, axis=1), local_picked]), "seq")
     log_total = row_top + jnp.log(row_total)
     probs = shifted / row_total[:, None]
     row_loss = log_total - picked
-    loss_value = lax.psum(jnp.sum(mask_float * row_loss), "dp") / num_valid
+    loss_value = total(jnp.sum(mask_float * row_loss).reshape(1), "dp")[0] / num_valid
     dlogits = ((probs - one_hot) * (mask_float / num_valid)[:, None]).astype(jnp.bfloat16)
-    shard_rows = lax.all_gather(dlogits, "dp", axis=0, tiled=True)
+    shard_rows = spread_all(dlogits, "dp").reshape(-1, vocab_rows)
     grad_slices = jnp.dot(shard_rows, head_weight, preferred_element_type=jnp.float32)
     grad_head = lax.dot_general(
         shard_rows, slices, (((0,), (0,)), ((), ())), preferred_element_type=jnp.float32
     )
     returned = lax.all_to_all(grad_slices, "dp", split_axis=0, concat_axis=1, tiled=True)
-    grad_normed = lax.psum(returned, "seq")
-    grad_gain = lax.psum(jnp.sum(grad_normed * unit_rows, axis=0), "dp")
+    mine = scatter_sum(returned, "seq")
+    grad_normed = spread_all(mine, "seq").reshape(returned.shape)
+    grad_gain = total(jnp.sum(grad_normed * unit_rows, axis=0), "dp")
     grad_hidden = norm_back(grad_normed, unit_rows, inv_rms, gain).astype(jnp.bfloat16)
     return (loss_value, grad_hidden, grad_gain, grad_head)
 

time: 836 us -> 568 us (0.68)
  waiting for transfers between devices: 445 us -> 185 us
  blocking collectives: 228 us -> 195 us
  starting transfers between devices: 0.13 us -> 21.5 us
  between operations: 14.5 us -> 1.4 us
  local copies, waits for them, and re-layouts: 5.84 us -> 17.7 us
    psum x1 -> x0, waiting for transfers between devices: 219 us -> none  [general(): grad_normed = lax.psum(returned, 'seq')]
    all_to_all x0 -> x5, waiting for transfers between devices: none -> 185 us  [the longest x1 121 us: scatter_sum(): parts = lax.all_to_all(x, name, split_axis=0, concat_axis=0, tiled=True)]
    all_to_all x0 -> x4, blocking collectives: none -> 143 us  [the longest x3 87.4 us: spread_all(): return lax.all_to_all(copies, name, split_axis=0, concat_axis=0, tiled=True)]
    reduce_scatter x1 -> x0, waiting for transfers between devices: 141 us -> none  [general(): lax.psum_scatter(lax.dot_general(slices, head_weight, NT, preferred_eleme...]
    psum x3 -> x0, blocking collectives: 118 us -> none  [the longest x1 53 us: general(): lax.psum((jnp.sum(shifted, axis=1), local_picked), 'seq')]
    all_gather x1 -> x0, waiting for transfers between devices: 85 us -> none  [general(): shard_rows = lax.all_gather(dlogits, 'dp', axis=0, tiled=True)]
    pmax x1 -> x0, blocking collectives: 55.2 us -> none  [general(): row_top = lax.pmax(jnp.max(logits, axis=1), 'seq')]
    all_to_all x0 -> x5, starting transfers between devices: none -> 21.5 us  [the longest x4 16.3 us: spread_all(): return lax.all_to_all(copies, name, split_axis=0, concat_axis=0, tiled=True)]
  transfers between devices with their start and end apart: 3 -> 5, of which waited for: 3 -> 5; matrix products, arithmetic and copies ran while one was open for 1% -> 2% of each run, Pallas kernels for 0% -> 0%
where the time goes in v4:
time: 568 us; the launch traced here: 565 us
  blocking collectives  195 us (34%)
  waiting for transfers between devices  185 us (33%)
  Pallas kernels  111 us (20%)
  starting transfers between devices  21.5 us (4%)
  local copies, waits for them, and re-layouts  17.7 us (3%)
  matrix products  17.5 us (3%)
  other arithmetic  14.5 us (3%)
    all_to_all x1, waiting for transfers between devices, scatter_sum(): parts = lax.all_to_all(x, name, split_axis=0, concat_axis=0, tiled=True)  121 us
    pallas_call x1, Pallas kernels, fused(): pl.pallas_call(kernel, out_shape=(jax.ShapeDtypeStruct((VP, CAP), BF16),...  111 us
    all_to_all x3, blocking collectives, spread_all(): return lax.all_to_all(copies, name, split_axis=0, concat_axis=0, tiled=True)  87.4 us
    all_to_all x4, waiting for transfers between devices, spread_all(): return lax.all_to_all(copies, name, split_axis=0, concat_axis=0, tiled=True)  63.4 us
    all_to_all x1, blocking collectives, scatter_sum(): parts = lax.all_to_all(x, name, split_axis=0, concat_axis=0, tiled=True)  55.7 us
    all_to_all x1, blocking collectives, general(): lax.all_to_all(grad_slices, 'dp', split_axis=0, concat_axis=1, tiled=True)  29 us
    all_to_all x1, blocking collectives, general(): lax.all_to_all(normed, 'dp', split_axis=1, concat_axis=0, tiled=True)  22.9 us
    all_to_all x4, starting transfers between devices, spread_all(): return lax.all_to_all(copies, name, split_axis=0, concat_axis=0, tiled=True)  16.3 us
  transfers between devices with their start and end apart: 5, of which 5 were waited for; matrix products, arithmetic and copies ran while one was open for 2% of the time, Pallas kernels for 0%

profile of v4, /device:TPU:0, one launch (start us, length us, event | category | flops | bytes accessed | tf_op | source)
XLA Modules:
  0.0 565.3 jit_solution(11572532330287281674)
XLA Ops:
  0.7 111.0 %fused.1 = (bf16[2688,640]{1,0:T(8,128)(2,1)S(1)}, bf16[640,512]{1,0:T(8,128)(2,1)S(1)}, bf16[128,4096]{1,0:T(8,128)(2,1)S(1)}, f32[32,128]{1,0:T(8,128)S(1)}, f32[1,1]{1,0:T(1,128)}, /*index=5*/s32[1,1]{1,0:T(1,128)}) custom-call(bf16[128,4096]{1,0:T(8,128)(2,1)} %hid_in.1, f32[32,128]{1,0:T(8,128)} %bitcast.37, bf16[2632,512]{1,0:T(8,128)(2,1)} %wgt_in.1, ...), custom_call_target="tpu_custom_call" | custom-call | flops 5174722560 | bytes 16777216 | tf_op jit(solution)/shard_map/fused/pallas_call | solution.py:500
  112.4 451.9 %conditional.1 = (f32[2632,512]{1,0:T(8,128)}, f32[]{:T(128)}, f32[4096]{0:T(1024)S(1)}, bf16[128,4096]{1,0:T(8,128)(2,1)S(1)}) conditional(s32[]{:T(128)} %bitcast.15, (bf16[2688,640]{1,0:T(8,128)(2,1)S(1)}, bf16[640,512]{1,0:T(8,128)(2,1)S(1)}, bf16[128,4096]{1,0:T(8,128)(2,1)S(1)}, f32[32,128]{1,0:T(8,128)S(1)}, f32[1,1]{1,0:T(1,128)}) %tuple.15, ...), branch_computations={%region_0.0_spmd, %region_1.0_spmd} | conditional | flops 8297851904 | bytes 194787232 | solution.py:632
  112.4 0.7 copy.42
  113.1 0.6 fusion.14
  113.6 0.7 fusion.8
  114.3 0.5 copy.33
  114.9 22.9 %all_to_all.68 = bf16[128,8,512]{2,0,1:T(8,128)(2,1)S(1)} all-to-all(bf16[128,8,512]{2,0,1:T(8,128)(2,1)S(1)} %copy.33), channel_id=1, replica_groups=mesh['dp'=8,'seq'=32] {'dp'}, dimensions={1} | all-to-all | bytes 2097152 | tf_op jit(solution)/shard_map/cond/branch_1_fun/all_to_all | solution.py:597
  137.7 1.0 copy-done.2
  138.7 7.3 %fusion.2 = f32[8,128,2632]{1,2,0:T(8,128)} fusion(bf16[2632,512]{1,0:T(8,128)(2,1)} %get-tuple-element.32, bf16[128,8,512]{2,0,1:T(8,128)(2,1)S(1)} %all_to_all.68), kind=kOutput, calls=%fused_computation.3 | convolution fusion | flops 2759852032 | bytes 14524416 | tf_op jit(solution)/shard_map/cond/branch_1_fun/dot_general | solution.py:600
  146.0 5.2 all-to-all-start.1
  151.2 121.4 %all-to-all-done.1 = f32[8,128,2632]{1,2,0:T(8,128)} async-done(((f32[8,128,2632]{1,2,0:T(8,128)}), f32[8,128,2632]{1,2,0:T(8,128)}, u32[]{:S(2)}, u32[]{:S(2)}) %all-to-all-start.1) | async-done | bytes 10780704 | tf_op jit(solution)/shard_map/cond/branch_1_fun/all_to_all | solution.py:582
  272.6 4.7 reduce_sum.105
  277.4 0.4 reduce_max.16
  277.7 0.6 broadcast_in_dim.0
  278.3 5.6 all-to-all-start.2
  284.0 8.0 %all-to-all-done.2 = f32[32,1,128]{2,1,0:T(1,128)S(1)} async-done(((f32[32,1,128]{2,1,0:T(1,128)}), f32[32,1,128]{2,1,0:T(1,128)S(1)}, u32[]{:S(2)}, u32[]{:S(2)}) %all-to-all-start.2) | async-done | bytes 16416 | tf_op jit(solution)/shard_map/cond/branch_1_fun/all_to_all | solution.py:577
  292.0 1.2 fusion.19
  293.2 11.3 %all_to_all.69 = f32[32,2,128]{2,1,0:T(2,128)S(1)} all-to-all(f32[32,2,128]{2,1,0:T(2,128)S(1)} %broadcast_in_dim.1), channel_id=1, replica_groups=mesh['dp'=8,'seq'=32] {'seq'}, dimensions={0} | all-to-all | bytes 65536 | tf_op jit(solution)/shard_map/cond/branch_1_fun/all_to_all | solution.py:577
  304.5 0.6 fusion.23
  305.1 0.6 broadcast_in_dim.3
  305.8 10.4 %all_to_all.70 = f32[8,1,1]{2,1,0:T(1,128)S(1)} all-to-all(f32[8,1,1]{2,1,0:T(1,128)S(1)} %broadcast_in_dim.3), channel_id=1, replica_groups=mesh['dp'=8,'seq'=32] {'dp'}, dimensions={0} | all-to-all | bytes 64 | tf_op jit(solution)/shard_map/cond/branch_1_fun/all_to_all | solution.py:577
  316.2 0.6 reduce_sum.112
  316.8 0.6 convert_divide_fusion
  317.4 1.2 fusion.18
  318.6 0.7 broadcast_in_dim.4
  319.3 65.7 %all_to_all.71 = bf16[8,128,2632]{1,2,0:T(8,128)(2,1)S(1)} all-to-all(bf16[8,128,2632]{1,2,0:T(8,128)(2,1)S(1)} %broadcast_in_dim.4), channel_id=1, replica_groups=mesh['dp'=8,'seq'=32] {'dp'}, dimensions={0} | all-to-all | bytes 10780672 | tf_op jit(solution)/shard_map/cond/branch_1_fun/all_to_all | solution.py:577
  385.0 3.5 fusion
  388.5 29.0 %all_to_all.72 = f32[8,128,512]{2,1,0:T(8,128)S(1)} all-to-all(f32[8,128,512]{2,1,0:T(8,128)S(1)} %fusion), channel_id=1, replica_groups=mesh['dp'=8,'seq'=32] {'dp'}, dimensions={0} | all-to-all | bytes 4194304 | tf_op jit(solution)/shard_map/cond/branch_1_fun/all_to_all | solution.py:617
  417.5 1.2 copy.37
  418.7 2.4 all_to_all.53
  421.2 55.7 %all_to_all.73 = f32[32,4,4096]{2,1,0:T(4,128)S(1)} all-to-all(f32[32,4,4096]{2,1,0:T(4,128)} %all_to_all.53), channel_id=1, replica_groups=mesh['dp'=8,'seq'=32] {'seq'}, dimensions={0} | all-to-all | bytes 4194304 | tf_op jit(solution)/shard_map/cond/branch_1_fun/all_to_all | solution.py:582
  476.9 1.2 broadcast_in_dim.2
  478.1 3.3 all-to-all-start.4
  481.8 7.2 %all-to-all-done.4 = f32[8,1,1]{2,1,0:T(1,128)S(1)} async-done(((f32[8,1,1]{2,1,0:T(1,128)}), f32[8,1,1]{2,1,0:T(1,128)S(1)}, u32[]{:S(2)}, u32[]{:S(2)}) %all-to-all-start.4) | async-done | bytes 64 | tf_op jit(solution)/shard_map/cond/branch_1_fun/all_to_all | solution.py:577
  488.9 1.8 broadcast_in_dim.5
  490.8 4.0 all-to-all-start.9
  494.8 0.6 reduce_sum.110
  496.6 6.7 %convolution_bitcast_fusion = f32[2632,512]{1,0:T(8,128)} fusion(bf16[8,128,2632]{1,2,0:T(8,128)(2,1)} %copy-done, bf16[128,8,512]{2,0,1:T(8,128)(2,1)} %copy-done.2), kind=kOutput, calls=%fused_computation | convolution fusion | flops 2759852032 | bytes 11829248 | tf_op jit(solution)/shard_map/cond/branch_1_fun/dot_general | solution.py:614
  503.4 43.1 %all-to-all-done.9 = f32[32,4,4096]{2,1,0:T(4,128)S(1)} async-done(((f32[32,4,4096]{2,1,0:T(4,128)}), f32[32,4,4096]{2,1,0:T(4,128)S(1)}, u32[]{:S(2)}, u32[]{:S(2)}) %all-to-all-start.9) | async-done | bytes 2097184 | tf_op jit(solution)/shard_map/cond/branch_1_fun/all_to_all | solution.py:577
  546.5 1.8 reshape.161
  548.2 1.9 copy.38
  550.2 1.3 fusion.9
  551.5 0.7 broadcast_in_dim.6
  552.2 3.4 all-to-all-start.10
  555.5 1.5 fusion.12
  557.0 1.5 copy.45
  558.5 5.1 all-to-all-done.10
  564.3 1.0 copy-done.7
  (26 shorter events, 0.6 us)
Async XLA Ops:
  0.6 111.7 %copy-start.1 = (bf16[128,4096]{1,0:T(8,128)(2,1)S(1)}, bf16[128,4096]{1,0:T(8,128)(2,1)}, u32[]{:S(2)}) copy-start(bf16[128,4096]{1,0:T(8,128)(2,1)} %hid_in.1) | copy-start | bytes 3145732
  0.6 111.7 %copy-start.3 = (f32[4096]{0:T(1024)S(1)}, f32[4096]{0:T(1024)}, u32[]{:S(2)}) copy-start(f32[4096]{0:T(1024)} %param.8) | copy-start | bytes 49156
  0.7 111.7 %copy-start.4 = (s32[128]{0:T(128)S(1)}, s32[128]{0:T(128)}, u32[]{:S(2)}) copy-start(s32[128]{0:T(128)} %param.10) | copy-start | bytes 1540
  0.7 111.7 %copy-start.5 = (s32[128]{0:T(128)S(1)}, s32[128]{0:T(128)}, u32[]{:S(2)}) copy-start(s32[128]{0:T(128)} %param.11) | copy-start | bytes 1540
  137.7 1.0 copy-start.2
  146.0 126.6 %all-to-all-start.1 = ((f32[8,128,2632]{1,2,0:T(8,128)}), f32[8,128,2632]{1,2,0:T(8,128)}, u32[]{:S(2)}, u32[]{:S(2)}) async-start(f32[8,128,2632]{1,2,0:T(8,128)} %fusion.2), calls=%async_computation.1 | async-start | bytes 21561344 | tf_op jit(solution)/shard_map/cond/branch_1_fun/all_to_all | solution.py:582
  278.3 13.6 %all-to-all-start.2 = ((f32[32,1,128]{2,1,0:T(1,128)}), f32[32,1,128]{2,1,0:T(1,128)S(1)}, u32[]{:S(2)}, u32[]{:S(2)}) async-start(f32[32,1,128]{2,1,0:T(1,128)} %broadcast_in_dim.0), calls=%async_computation.2 | async-start | bytes 32768 | tf_op jit(solution)/shard_map/cond/branch_1_fun/all_to_all | solution.py:577
  319.3 65.7 %copy-start.6 = (bf16[2632,512]{1,0:T(8,128)(2,1)S(1)}, bf16[2632,512]{1,0:T(8,128)(2,1)}, u32[]{:S(2)}) copy-start(bf16[2632,512]{1,0:T(8,128)(2,1)} %get-tuple-element.32) | copy-start | bytes 8085508 | tf_op jit(solution)/shard_map/cond
  385.0 3.5 copy-start
  478.1 10.8 %all-to-all-start.4 = ((f32[8,1,1]{2,1,0:T(1,128)}), f32[8,1,1]{2,1,0:T(1,128)S(1)}, u32[]{:S(2)}, u32[]{:S(2)}) async-start(f32[8,1,1]{2,1,0:T(1,128)} %broadcast_in_dim.2), calls=%async_computation.4 | async-start | bytes 8192 | tf_op jit(solution)/shard_map/cond/branch_1_fun/all_to_all | solution.py:577
  490.8 55.7 %all-to-all-start.9 = ((f32[32,4,4096]{2,1,0:T(4,128)}), f32[32,4,4096]{2,1,0:T(4,128)S(1)}, u32[]{:S(2)}, u32[]{:S(2)}) async-start(f32[32,4,4096]{2,1,0:T(4,128)} %broadcast_in_dim.5), calls=%async_computation.9 | async-start | bytes 4194304 | tf_op jit(solution)/shard_map/cond/branch_1_fun/all_to_all | solution.py:577
  552.2 11.5 %all-to-all-start.10 = ((f32[8,1,4096]{2,1,0:T(1,128)}), f32[8,1,4096]{2,1,0:T(1,128)S(1)}, u32[]{:S(2)}, u32[]{:S(2)}) async-start(f32[8,1,4096]{2,1,0:T(1,128)} %broadcast_in_dim.6), calls=%async_computation.10 | async-start | bytes 262144 | tf_op jit(solution)/shard_map/cond/branch_1_fun/all_to_all | solution.py:577
  564.3 1.0 copy-start.7
  564.3 1.0 copy-start.8

commit v5 on v4

--- a/solution.py
+++ b/solution.py
@@ -37,7 +37,7 @@
 H0, M0, HC0 = sems(8), sems(8), sems(8)
 S10, S20, S30, G30, G20, G10 = [sems(CH) for _ in range(6)]
 T10, T20, T30 = sems(4), sems(8), sems(8)
-DC0, DX0, DZ0, DP0, AZ0, AX0, AC0 = sems(1), sems(8), sems(8), sems(8), sems(8), sems(8), sems(16)
+DC0, DX0, DZ0, DP0, AZ0, AX0, AC0 = sems(2), sems(8), sems(8), sems(8), sems(8), sems(8), sems(16)
 
 
 def kernel(hid_in, gain, wgt_in, tgt, msk, dlo, C, ghid, gg, scal, flag,
@@ -339,23 +339,29 @@
         dlo[rows, :] = dl.astype(BF16)
         DN[...] += jnp.dot(WT[i], dlo[rows, :], preferred_element_type=F32)
 
-    dc = rcopy(DN.at[rows_at((1 - co) * 256, 256), :], RC, DC0, core_dev)
-    dc.start()
-    dc.wait_recv()
-    T1[...] = DN[rows_at(co * 256, 256), :] + RC[...]
+    pass_on, keep = (1 - xl) * 128, xl * 128
+    dc = []
+    for n, start in enumerate((pass_on, keep)):
+        c = rcopy(DN.at[rows_at((1 - co) * 256 + start, 128), :], RC.at[rows_at(start, 128), :], DC0 + n, core_dev)
+        c.start()
+        dc.append(c)
+    dc[0].wait_recv()
     far = (4, 3, 5, 2, 6, 1, 7, 0)
     dx = []
     for n, k in enumerate(far):
         zz = lax.rem(z + k, 8)
-        B1[zz] = T1[rows_at((1 - xl) * 128 + zz * 16, 16), :]
+        at = pass_on + zz * 16
+        B1[zz] = DN[rows_at(co * 256 + at, 16), :] + RC[rows_at(at, 16), :]
         c = rcopy(B1.at[zz], RX.at[zz], DX0 + n, xlo_dev)
         c.start()
         dx.append(c)
+    dc[1].wait_recv()
+    T1[...] = DN[rows_at(co * 256 + keep, 128), :] + RC[rows_at(keep, 128), :]
     dz = []
     for n, k in enumerate(far):
         zz = lax.rem(z + k, 8)
         dx[n].wait_recv()
-        part = T1[rows_at(xl * 128 + zz * 16, 16), :] + RX[zz]
+        part = T1[rows_at(zz * 16, 16), :] + RX[zz]
         if k:
             B2[zz] = part
             c = rcopy(B2.at[zz], RZ.at[z], DZ0 + k, (dp, seq_of(zz, xl, co)))
@@ -445,7 +451,7 @@
         slice_copy(oc * 16 + ox * 8 + (z_from[k - 1] if k else z), AC0 + 8 + k, (dp, seq)).wait_recv()
     emit(oc, ox)
 
-    for c in hsend + msend + hc + sends + [dc] + dx + dz + dpc:
+    for c in hsend + msend + hc + sends + dc + dx + dz + dpc:
         c.wait_send()
 
     @pl.loop(0, CH)
@@ -486,7 +492,7 @@
         pltpu.VMEM((VP, CAP), BF16),
         pltpu.VMEM((W, CAP), F32),
         pltpu.VMEM((256, CAP), F32),
-        pltpu.VMEM((256, CAP), F32),
+        pltpu.VMEM((128, CAP), F32),
         pltpu.VMEM((8, 16, CAP), F32),
         pltpu.VMEM((8, 16, CAP), F32),
         pltpu.VMEM((8, 16, CAP), F32),
@@ -517,7 +523,7 @@
     )(hidden, gain.reshape(32, B), head_weight, targets.reshape(1, B), loss_mask.reshape(1, B))
 
 
-STEPS = 8
+STEPS = 4
 
 
 def finish_kernel(dl, c, ghid, gg, scal, gh, ghid_out, gg_out, loss, fs):

time: 568 us -> 567 us (level)
  no operation moved by 1% of the time
where the time goes in v5:
time: 567 us; the launch traced here: 565 us
  blocking collectives  195 us (34%)
  waiting for transfers between devices  185 us (33%)
  Pallas kernels  111 us (20%)
  starting transfers between devices  21.4 us (4%)
  local copies, waits for them, and re-layouts  17.7 us (3%)
  matrix products  17.5 us (3%)
  other arithmetic  14.5 us (3%)
    all_to_all x1, waiting for transfers between devices, scatter_sum(): parts = lax.all_to_all(x, name, split_axis=0, concat_axis=0, tiled=True)  121 us
    pallas_call x1, Pallas kernels, fused(): pl.pallas_call(kernel, out_shape=(jax.ShapeDtypeStruct((VP, CAP), BF16),...  111 us
    all_to_all x3, blocking collectives, spread_all(): return lax.all_to_all(copies, name, split_axis=0, concat_axis=0, tiled=True)  87.3 us
    all_to_all x4, waiting for transfers between devices, spread_all(): return lax.all_to_all(copies, name, split_axis=0, concat_axis=0, tiled=True)  63.4 us
    all_to_all x1, blocking collectives, scatter_sum(): parts = lax.all_to_all(x, name, split_axis=0, concat_axis=0, tiled=True)  55.7 us
    all_to_all x1, blocking collectives, general(): lax.all_to_all(grad_slices, 'dp', split_axis=0, concat_axis=1, tiled=True)  29 us
    all_to_all x1, blocking collectives, general(): lax.all_to_all(normed, 'dp', split_axis=1, concat_axis=0, tiled=True)  22.6 us
    all_to_all x4, starting transfers between devices, spread_all(): return lax.all_to_all(copies, name, split_axis=0, concat_axis=0, tiled=True)  16.2 us
  transfers between devices with their start and end apart: 5, of which 5 were waited for; matrix products, arithmetic and copies ran while one was open for 2% of the time, Pallas kernels for 0%

profile of v5, /device:TPU:0, one launch (start us, length us, event | category | flops | bytes accessed | tf_op | source)
XLA Modules:
  0.0 564.7 jit_solution(5605460769633134674)
XLA Ops:
  0.7 110.8 %fused.1 = (bf16[2688,640]{1,0:T(8,128)(2,1)S(1)}, bf16[640,512]{1,0:T(8,128)(2,1)S(1)}, bf16[128,4096]{1,0:T(8,128)(2,1)S(1)}, f32[32,128]{1,0:T(8,128)S(1)}, f32[1,1]{1,0:T(1,128)}, /*index=5*/s32[1,1]{1,0:T(1,128)}) custom-call(bf16[128,4096]{1,0:T(8,128)(2,1)} %hid_in.1, f32[32,128]{1,0:T(8,128)} %bitcast.37, bf16[2632,512]{1,0:T(8,128)(2,1)} %wgt_in.1, ...), custom_call_target="tpu_custom_call" | custom-call | flops 5174722560 | bytes 16777216 | tf_op jit(solution)/shard_map/fused/pallas_call | solution.py:506
  112.2 451.5 %conditional.1 = (f32[2632,512]{1,0:T(8,128)}, f32[]{:T(128)}, f32[4096]{0:T(1024)S(1)}, bf16[128,4096]{1,0:T(8,128)(2,1)S(1)}) conditional(s32[]{:T(128)} %bitcast.15, (bf16[2688,640]{1,0:T(8,128)(2,1)S(1)}, bf16[640,512]{1,0:T(8,128)(2,1)S(1)}, bf16[128,4096]{1,0:T(8,128)(2,1)S(1)}, f32[32,128]{1,0:T(8,128)S(1)}, f32[1,1]{1,0:T(1,128)}) %tuple.15, ...), branch_computations={%region_0.0_spmd, %region_1.0_spmd} | conditional | flops 8297851904 | bytes 194787232 | solution.py:638
  112.2 0.7 copy.42
  112.9 0.6 fusion.14
  113.5 0.7 fusion.8
  114.2 0.5 copy.33
  114.7 22.6 %all_to_all.68 = bf16[128,8,512]{2,0,1:T(8,128)(2,1)S(1)} all-to-all(bf16[128,8,512]{2,0,1:T(8,128)(2,1)S(1)} %copy.33), channel_id=1, replica_groups=mesh['dp'=8,'seq'=32] {'dp'}, dimensions={1} | all-to-all | bytes 2097152 | tf_op jit(solution)/shard_map/cond/branch_1_fun/all_to_all | solution.py:603
  137.3 1.0 copy-done.2
  138.3 7.3 %fusion.2 = f32[8,128,2632]{1,2,0:T(8,128)} fusion(bf16[2632,512]{1,0:T(8,128)(2,1)} %get-tuple-element.32, bf16[128,8,512]{2,0,1:T(8,128)(2,1)S(1)} %all_to_all.68), kind=kOutput, calls=%fused_computation.3 | convolution fusion | flops 2759852032 | bytes 14524416 | tf_op jit(solution)/shard_map/cond/branch_1_fun/dot_general | solution.py:606
  145.6 5.2 all-to-all-start.1
  150.8 121.4 %all-to-all-done.1 = f32[8,128,2632]{1,2,0:T(8,128)} async-done(((f32[8,128,2632]{1,2,0:T(8,128)}), f32[8,128,2632]{1,2,0:T(8,128)}, u32[]{:S(2)}, u32[]{:S(2)}) %all-to-all-start.1) | async-done | bytes 10780704 | tf_op jit(solution)/shard_map/cond/branch_1_fun/all_to_all | solution.py:588
  272.2 4.7 reduce_sum.105
  277.0 0.4 reduce_max.16
  277.3 0.6 broadcast_in_dim.0
  277.9 5.5 all-to-all-start.2
  283.5 8.0 %all-to-all-done.2 = f32[32,1,128]{2,1,0:T(1,128)S(1)} async-done(((f32[32,1,128]{2,1,0:T(1,128)}), f32[32,1,128]{2,1,0:T(1,128)S(1)}, u32[]{:S(2)}, u32[]{:S(2)}) %all-to-all-start.2) | async-done | bytes 16416 | tf_op jit(solution)/shard_map/cond/branch_1_fun/all_to_all | solution.py:583
  291.5 1.2 fusion.19
  292.7 11.3 %all_to_all.69 = f32[32,2,128]{2,1,0:T(2,128)S(1)} all-to-all(f32[32,2,128]{2,1,0:T(2,128)S(1)} %broadcast_in_dim.1), channel_id=1, replica_groups=mesh['dp'=8,'seq'=32] {'seq'}, dimensions={0} | all-to-all | bytes 65536 | tf_op jit(solution)/shard_map/cond/branch_1_fun/all_to_all | solution.py:583
  304.0 0.6 fusion.23
  304.6 0.6 broadcast_in_dim.3
  305.3 10.4 %all_to_all.70 = f32[8,1,1]{2,1,0:T(1,128)S(1)} all-to-all(f32[8,1,1]{2,1,0:T(1,128)S(1)} %broadcast_in_dim.3), channel_id=1, replica_groups=mesh['dp'=8,'seq'=32] {'dp'}, dimensions={0} | all-to-all | bytes 64 | tf_op jit(solution)/shard_map/cond/branch_1_fun/all_to_all | solution.py:583
  315.7 0.6 reduce_sum.112
  316.3 0.6 convert_divide_fusion
  316.8 1.2 fusion.18
  318.1 0.7 broadcast_in_dim.4
  318.8 65.7 %all_to_all.71 = bf16[8,128,2632]{1,2,0:T(8,128)(2,1)S(1)} all-to-all(bf16[8,128,2632]{1,2,0:T(8,128)(2,1)S(1)} %broadcast_in_dim.4), channel_id=1, replica_groups=mesh['dp'=8,'seq'=32] {'dp'}, dimensions={0} | all-to-all | bytes 10780672 | tf_op jit(solution)/shard_map/cond/branch_1_fun/all_to_all | solution.py:583
  384.5 3.5 fusion
  388.0 29.0 %all_to_all.72 = f32[8,128,512]{2,1,0:T(8,128)S(1)} all-to-all(f32[8,128,512]{2,1,0:T(8,128)S(1)} %fusion), channel_id=1, replica_groups=mesh['dp'=8,'seq'=32] {'dp'}, dimensions={0} | all-to-all | bytes 4194304 | tf_op jit(solution)/shard_map/cond/branch_1_fun/all_to_all | solution.py:623
  417.0 1.2 copy.37
  418.2 2.4 all_to_all.53
  420.6 55.7 %all_to_all.73 = f32[32,4,4096]{2,1,0:T(4,128)S(1)} all-to-all(f32[32,4,4096]{2,1,0:T(4,128)} %all_to_all.53), channel_id=1, replica_groups=mesh['dp'=8,'seq'=32] {'seq'}, dimensions={0} | all-to-all | bytes 4194304 | tf_op jit(solution)/shard_map/cond/branch_1_fun/all_to_all | solution.py:588
  476.3 1.2 broadcast_in_dim.2
  477.6 3.3 all-to-all-start.4
  481.2 7.2 %all-to-all-done.4 = f32[8,1,1]{2,1,0:T(1,128)S(1)} async-done(((f32[8,1,1]{2,1,0:T(1,128)}), f32[8,1,1]{2,1,0:T(1,128)S(1)}, u32[]{:S(2)}, u32[]{:S(2)}) %all-to-all-start.4) | async-done | bytes 64 | tf_op jit(solution)/shard_map/cond/branch_1_fun/all_to_all | solution.py:583
  488.4 1.8 broadcast_in_dim.5
  490.2 4.0 all-to-all-start.9
  494.2 0.6 reduce_sum.110
  496.1 6.7 %convolution_bitcast_fusion = f32[2632,512]{1,0:T(8,128)} fusion(bf16[8,128,2632]{1,2,0:T(8,128)(2,1)} %copy-done, bf16[128,8,512]{2,0,1:T(8,128)(2,1)} %copy-done.2), kind=kOutput, calls=%fused_computation | convolution fusion | flops 2759852032 | bytes 11829248 | tf_op jit(solution)/shard_map/cond/branch_1_fun/dot_general | solution.py:620
  502.8 43.1 %all-to-all-done.9 = f32[32,4,4096]{2,1,0:T(4,128)S(1)} async-done(((f32[32,4,4096]{2,1,0:T(4,128)}), f32[32,4,4096]{2,1,0:T(4,128)S(1)}, u32[]{:S(2)}, u32[]{:S(2)}) %all-to-all-start.9) | async-done | bytes 2097184 | tf_op jit(solution)/shard_map/cond/branch_1_fun/all_to_all | solution.py:583
  546.0 1.8 reshape.161
  547.7 1.9 copy.38
  549.6 1.3 fusion.9
  550.9 0.7 broadcast_in_dim.6
  551.6 3.4 all-to-all-start.10
  555.0 1.5 fusion.12
  556.5 1.5 copy.45
  558.0 5.1 all-to-all-done.10
  563.8 1.0 copy-done.7
  (26 shorter events, 0.6 us)
Async XLA Ops:
  0.6 111.5 %copy-start.1 = (bf16[128,4096]{1,0:T(8,128)(2,1)S(1)}, bf16[128,4096]{1,0:T(8,128)(2,1)}, u32[]{:S(2)}) copy-start(bf16[128,4096]{1,0:T(8,128)(2,1)} %hid_in.1) | copy-start | bytes 3145732
  0.6 111.5 %copy-start.3 = (f32[4096]{0:T(1024)S(1)}, f32[4096]{0:T(1024)}, u32[]{:S(2)}) copy-start(f32[4096]{0:T(1024)} %param.8) | copy-start | bytes 49156
  0.7 111.5 %copy-start.4 = (s32[128]{0:T(128)S(1)}, s32[128]{0:T(128)}, u32[]{:S(2)}) copy-start(s32[128]{0:T(128)} %param.10) | copy-start | bytes 1540
  0.7 111.5 %copy-start.5 = (s32[128]{0:T(128)S(1)}, s32[128]{0:T(128)}, u32[]{:S(2)}) copy-start(s32[128]{0:T(128)} %param.11) | copy-start | bytes 1540
  137.3 1.0 copy-start.2
  145.6 126.6 %all-to-all-start.1 = ((f32[8,128,2632]{1,2,0:T(8,128)}), f32[8,128,2632]{1,2,0:T(8,128)}, u32[]{:S(2)}, u32[]{:S(2)}) async-start(f32[8,128,2632]{1,2,0:T(8,128)} %fusion.2), calls=%async_computation.1 | async-start | bytes 21561344 | tf_op jit(solution)/shard_map/cond/branch_1_fun/all_to_all | solution.py:588
  277.9 13.5 %all-to-all-start.2 = ((f32[32,1,128]{2,1,0:T(1,128)}), f32[32,1,128]{2,1,0:T(1,128)S(1)}, u32[]{:S(2)}, u32[]{:S(2)}) async-start(f32[32,1,128]{2,1,0:T(1,128)} %broadcast_in_dim.0), calls=%async_computation.2 | async-start | bytes 32768 | tf_op jit(solution)/shard_map/cond/branch_1_fun/all_to_all | solution.py:583
  318.8 65.7 %copy-start.6 = (bf16[2632,512]{1,0:T(8,128)(2,1)S(1)}, bf16[2632,512]{1,0:T(8,128)(2,1)}, u32[]{:S(2)}) copy-start(bf16[2632,512]{1,0:T(8,128)(2,1)} %get-tuple-element.32) | copy-start | bytes 8085508 | tf_op jit(solution)/shard_map/cond
  384.5 3.5 copy-start
  477.6 10.8 %all-to-all-start.4 = ((f32[8,1,1]{2,1,0:T(1,128)}), f32[8,1,1]{2,1,0:T(1,128)S(1)}, u32[]{:S(2)}, u32[]{:S(2)}) async-start(f32[8,1,1]{2,1,0:T(1,128)} %broadcast_in_dim.2), calls=%async_computation.4 | async-start | bytes 8192 | tf_op jit(solution)/shard_map/cond/branch_1_fun/all_to_all | solution.py:583
  490.2 55.7 %all-to-all-start.9 = ((f32[32,4,4096]{2,1,0:T(4,128)}), f32[32,4,4096]{2,1,0:T(4,128)S(1)}, u32[]{:S(2)}, u32[]{:S(2)}) async-start(f32[32,4,4096]{2,1,0:T(4,128)} %broadcast_in_dim.5), calls=%async_computation.9 | async-start | bytes 4194304 | tf_op jit(solution)/shard_map/cond/branch_1_fun/all_to_all | solution.py:583
  551.6 11.5 %all-to-all-start.10 = ((f32[8,1,4096]{2,1,0:T(1,128)}), f32[8,1,4096]{2,1,0:T(1,128)S(1)}, u32[]{:S(2)}, u32[]{:S(2)}) async-start(f32[8,1,4096]{2,1,0:T(1,128)} %broadcast_in_dim.6), calls=%async_computation.10 | async-start | bytes 262144 | tf_op jit(solution)/shard_map/cond/branch_1_fun/all_to_all | solution.py:583
  563.8 1.0 copy-start.7
  563.8 1.0 copy-start.8

commit v6 on v5

--- a/solution.py
+++ b/solution.py
@@ -74,8 +74,6 @@
 
     fetch_hid = pltpu.make_async_copy(hid_in, hid, ls.at[0])
     fetch_hid.start()
-    fetch_wgt = pltpu.make_async_copy(wgt_in, wgt, ls.at[1])
-    fetch_wgt.start()
 
     barrier = pltpu.get_barrier_semaphore()
     for j in dp_peers:
@@ -86,6 +84,8 @@
         pl.semaphore_signal(barrier, inc=1, device_id=(dp, seq_of(zz, xl, co)), device_id_type=MESH)
 
     fetch_hid.wait()
+    fetch_wgt = pltpu.make_async_copy(wgt_in, wgt, ls.at[1])
+    fetch_wgt.start()
     total = jnp.zeros((B, 1), F32)
     for j in range(8):
         x = hid[:, j * W:(j + 1) * W].astype(F32)

time: 567 us -> 567 us (level)
  no operation moved by 1% of the time
where the time goes in v6:
time: 567 us; the launch traced here: 565 us
  blocking collectives  195 us (34%)
  waiting for transfers between devices  185 us (33%)
  Pallas kernels  111 us (20%)
  starting transfers between devices  20.8 us (4%)
  local copies, waits for them, and re-layouts  17.7 us (3%)
  matrix products  17.5 us (3%)
  other arithmetic  14.5 us (3%)
    all_to_all x1, waiting for transfers between devices, scatter_sum(): parts = lax.all_to_all(x, name, split_axis=0, concat_axis=0, tiled=True)  121 us
    pallas_call x1, Pallas kernels, fused(): pl.pallas_call(kernel, out_shape=(jax.ShapeDtypeStruct((VP, CAP), BF16),...  111 us
    all_to_all x3, blocking collectives, spread_all(): return lax.all_to_all(copies, name, split_axis=0, concat_axis=0, tiled=True)  87.3 us
    all_to_all x4, waiting for transfers between devices, spread_all(): return lax.all_to_all(copies, name, split_axis=0, concat_axis=0, tiled=True)  63.4 us
    all_to_all x1, blocking collectives, scatter_sum(): parts = lax.all_to_all(x, name, split_axis=0, concat_axis=0, tiled=True)  55.7 us
    all_to_all x1, blocking collectives, general(): lax.all_to_all(grad_slices, 'dp', split_axis=0, concat_axis=1, tiled=True)  29 us
    all_to_all x1, blocking collectives, general(): lax.all_to_all(normed, 'dp', split_axis=1, concat_axis=0, tiled=True)  23.1 us
    all_to_all x4, starting transfers between devices, spread_all(): return lax.all_to_all(copies, name, split_axis=0, concat_axis=0, tiled=True)  15.7 us
  transfers between devices with their start and end apart: 5, of which 5 were waited for; matrix products, arithmetic and copies ran while one was open for 2% of the time, Pallas kernels for 0%

profile of v6, /device:TPU:0, one launch (start us, length us, event | category | flops | bytes accessed | tf_op | source)
XLA Modules:
  0.0 564.7 jit_solution(10132897505251378671)
XLA Ops:
  0.7 110.8 %fused.1 = (bf16[2688,640]{1,0:T(8,128)(2,1)S(1)}, bf16[640,512]{1,0:T(8,128)(2,1)S(1)}, bf16[128,4096]{1,0:T(8,128)(2,1)S(1)}, f32[32,128]{1,0:T(8,128)S(1)}, f32[1,1]{1,0:T(1,128)}, /*index=5*/s32[1,1]{1,0:T(1,128)}) custom-call(bf16[128,4096]{1,0:T(8,128)(2,1)} %hid_in.1, f32[32,128]{1,0:T(8,128)} %bitcast.37, bf16[2632,512]{1,0:T(8,128)(2,1)} %wgt_in.1, ...), custom_call_target="tpu_custom_call" | custom-call | flops 5174722560 | bytes 16777216 | tf_op jit(solution)/shard_map/fused/pallas_call | solution.py:506
  112.3 451.5 %conditional.1 = (f32[2632,512]{1,0:T(8,128)}, f32[]{:T(128)}, f32[4096]{0:T(1024)S(1)}, bf16[128,4096]{1,0:T(8,128)(2,1)S(1)}) conditional(s32[]{:T(128)} %bitcast.15, (bf16[2688,640]{1,0:T(8,128)(2,1)S(1)}, bf16[640,512]{1,0:T(8,128)(2,1)S(1)}, bf16[128,4096]{1,0:T(8,128)(2,1)S(1)}, f32[32,128]{1,0:T(8,128)S(1)}, f32[1,1]{1,0:T(1,128)}) %tuple.15, ...), branch_computations={%region_0.0_spmd, %region_1.0_spmd} | conditional | flops 8297851904 | bytes 194787232 | solution.py:638
  112.3 0.7 copy.42
  112.9 0.6 fusion.14
  113.5 0.7 fusion.8
  114.2 0.5 copy.33
  114.8 23.1 %all_to_all.68 = bf16[128,8,512]{2,0,1:T(8,128)(2,1)S(1)} all-to-all(bf16[128,8,512]{2,0,1:T(8,128)(2,1)S(1)} %copy.33), channel_id=1, replica_groups=mesh['dp'=8,'seq'=32] {'dp'}, dimensions={1} | all-to-all | bytes 2097152 | tf_op jit(solution)/shard_map/cond/branch_1_fun/all_to_all | solution.py:603
  137.9 1.0 copy-done.2
  138.9 7.3 %fusion.2 = f32[8,128,2632]{1,2,0:T(8,128)} fusion(bf16[2632,512]{1,0:T(8,128)(2,1)} %get-tuple-element.32, bf16[128,8,512]{2,0,1:T(8,128)(2,1)S(1)} %all_to_all.68), kind=kOutput, calls=%fused_computation.3 | convolution fusion | flops 2759852032 | bytes 14524416 | tf_op jit(solution)/shard_map/cond/branch_1_fun/dot_general | solution.py:606
  146.2 5.2 all-to-all-start.1
  151.3 121.4 %all-to-all-done.1 = f32[8,128,2632]{1,2,0:T(8,128)} async-done(((f32[8,128,2632]{1,2,0:T(8,128)}), f32[8,128,2632]{1,2,0:T(8,128)}, u32[]{:S(2)}, u32[]{:S(2)}) %all-to-all-start.1) | async-done | bytes 10780704 | tf_op jit(solution)/shard_map/cond/branch_1_fun/all_to_all | solution.py:588
  272.8 4.7 reduce_sum.105
  277.5 0.4 reduce_max.16
  277.9 0.6 broadcast_in_dim.0
  278.5 5.0 all-to-all-start.2
  283.5 8.0 %all-to-all-done.2 = f32[32,1,128]{2,1,0:T(1,128)S(1)} async-done(((f32[32,1,128]{2,1,0:T(1,128)}), f32[32,1,128]{2,1,0:T(1,128)S(1)}, u32[]{:S(2)}, u32[]{:S(2)}) %all-to-all-start.2) | async-done | bytes 16416 | tf_op jit(solution)/shard_map/cond/branch_1_fun/all_to_all | solution.py:583
  291.5 1.2 fusion.19
  292.7 11.3 %all_to_all.69 = f32[32,2,128]{2,1,0:T(2,128)S(1)} all-to-all(f32[32,2,128]{2,1,0:T(2,128)S(1)} %broadcast_in_dim.1), channel_id=1, replica_groups=mesh['dp'=8,'seq'=32] {'seq'}, dimensions={0} | all-to-all | bytes 65536 | tf_op jit(solution)/shard_map/cond/branch_1_fun/all_to_all | solution.py:583
  304.0 0.6 fusion.23
  304.7 0.6 broadcast_in_dim.3
  305.3 10.4 %all_to_all.70 = f32[8,1,1]{2,1,0:T(1,128)S(1)} all-to-all(f32[8,1,1]{2,1,0:T(1,128)S(1)} %broadcast_in_dim.3), channel_id=1, replica_groups=mesh['dp'=8,'seq'=32] {'dp'}, dimensions={0} | all-to-all | bytes 64 | tf_op jit(solution)/shard_map/cond/branch_1_fun/all_to_all | solution.py:583
  315.7 0.6 reduce_sum.112
  316.3 0.6 convert_divide_fusion
  316.8 1.2 fusion.18
  318.1 0.7 broadcast_in_dim.4
  318.8 65.7 %all_to_all.71 = bf16[8,128,2632]{1,2,0:T(8,128)(2,1)S(1)} all-to-all(bf16[8,128,2632]{1,2,0:T(8,128)(2,1)S(1)} %broadcast_in_dim.4), channel_id=1, replica_groups=mesh['dp'=8,'seq'=32] {'dp'}, dimensions={0} | all-to-all | bytes 10780672 | tf_op jit(solution)/shard_map/cond/branch_1_fun/all_to_all | solution.py:583
  384.5 3.5 fusion
  388.0 29.0 %all_to_all.72 = f32[8,128,512]{2,1,0:T(8,128)S(1)} all-to-all(f32[8,128,512]{2,1,0:T(8,128)S(1)} %fusion), channel_id=1, replica_groups=mesh['dp'=8,'seq'=32] {'dp'}, dimensions={0} | all-to-all | bytes 4194304 | tf_op jit(solution)/shard_map/cond/branch_1_fun/all_to_all | solution.py:623
  417.0 1.2 copy.37
  418.2 2.4 all_to_all.53
  420.6 55.7 %all_to_all.73 = f32[32,4,4096]{2,1,0:T(4,128)S(1)} all-to-all(f32[32,4,4096]{2,1,0:T(4,128)} %all_to_all.53), channel_id=1, replica_groups=mesh['dp'=8,'seq'=32] {'seq'}, dimensions={0} | all-to-all | bytes 4194304 | tf_op jit(solution)/shard_map/cond/branch_1_fun/all_to_all | solution.py:588
  476.3 1.2 broadcast_in_dim.2
  477.6 3.3 all-to-all-start.4
  481.2 7.2 %all-to-all-done.4 = f32[8,1,1]{2,1,0:T(1,128)S(1)} async-done(((f32[8,1,1]{2,1,0:T(1,128)}), f32[8,1,1]{2,1,0:T(1,128)S(1)}, u32[]{:S(2)}, u32[]{:S(2)}) %all-to-all-start.4) | async-done | bytes 64 | tf_op jit(solution)/shard_map/cond/branch_1_fun/all_to_all | solution.py:583
  488.4 1.8 broadcast_in_dim.5
  490.2 4.0 all-to-all-start.9
  494.3 0.6 reduce_sum.110
  496.1 6.7 %convolution_bitcast_fusion = f32[2632,512]{1,0:T(8,128)} fusion(bf16[8,128,2632]{1,2,0:T(8,128)(2,1)} %copy-done, bf16[128,8,512]{2,0,1:T(8,128)(2,1)} %copy-done.2), kind=kOutput, calls=%fused_computation | convolution fusion | flops 2759852032 | bytes 11829248 | tf_op jit(solution)/shard_map/cond/branch_1_fun/dot_general | solution.py:620
  502.8 43.1 %all-to-all-done.9 = f32[32,4,4096]{2,1,0:T(4,128)S(1)} async-done(((f32[32,4,4096]{2,1,0:T(4,128)}), f32[32,4,4096]{2,1,0:T(4,128)S(1)}, u32[]{:S(2)}, u32[]{:S(2)}) %all-to-all-start.9) | async-done | bytes 2097184 | tf_op jit(solution)/shard_map/cond/branch_1_fun/all_to_all | solution.py:583
  546.0 1.8 reshape.161
  547.7 1.9 copy.38
  549.6 1.3 fusion.9
  550.9 0.7 broadcast_in_dim.6
  551.6 3.4 all-to-all-start.10
  555.0 1.5 fusion.12
  556.5 1.5 copy.45
  558.0 5.1 all-to-all-done.10
  563.8 1.0 copy-done.7
  (26 shorter events, 0.6 us)
Async XLA Ops:
  0.6 111.6 %copy-start.1 = (bf16[128,4096]{1,0:T(8,128)(2,1)S(1)}, bf16[128,4096]{1,0:T(8,128)(2,1)}, u32[]{:S(2)}) copy-start(bf16[128,4096]{1,0:T(8,128)(2,1)} %hid_in.1) | copy-start | bytes 3145732
  0.6 111.6 %copy-start.3 = (f32[4096]{0:T(1024)S(1)}, f32[4096]{0:T(1024)}, u32[]{:S(2)}) copy-start(f32[4096]{0:T(1024)} %param.8) | copy-start | bytes 49156
  0.7 111.6 %copy-start.4 = (s32[128]{0:T(128)S(1)}, s32[128]{0:T(128)}, u32[]{:S(2)}) copy-start(s32[128]{0:T(128)} %param.10) | copy-start | bytes 1540
  0.7 111.6 %copy-start.5 = (s32[128]{0:T(128)S(1)}, s32[128]{0:T(128)}, u32[]{:S(2)}) copy-start(s32[128]{0:T(128)} %param.11) | copy-start | bytes 1540
  137.9 1.0 copy-start.2
  146.2 126.6 %all-to-all-start.1 = ((f32[8,128,2632]{1,2,0:T(8,128)}), f32[8,128,2632]{1,2,0:T(8,128)}, u32[]{:S(2)}, u32[]{:S(2)}) async-start(f32[8,128,2632]{1,2,0:T(8,128)} %fusion.2), calls=%async_computation.1 | async-start | bytes 21561344 | tf_op jit(solution)/shard_map/cond/branch_1_fun/all_to_all | solution.py:588
  278.5 13.0 %all-to-all-start.2 = ((f32[32,1,128]{2,1,0:T(1,128)}), f32[32,1,128]{2,1,0:T(1,128)S(1)}, u32[]{:S(2)}, u32[]{:S(2)}) async-start(f32[32,1,128]{2,1,0:T(1,128)} %broadcast_in_dim.0), calls=%async_computation.2 | async-start | bytes 32768 | tf_op jit(solution)/shard_map/cond/branch_1_fun/all_to_all | solution.py:583
  318.8 65.7 %copy-start.6 = (bf16[2632,512]{1,0:T(8,128)(2,1)S(1)}, bf16[2632,512]{1,0:T(8,128)(2,1)}, u32[]{:S(2)}) copy-start(bf16[2632,512]{1,0:T(8,128)(2,1)} %get-tuple-element.32) | copy-start | bytes 8085508 | tf_op jit(solution)/shard_map/cond
  384.5 3.5 copy-start
  477.6 10.8 %all-to-all-start.4 = ((f32[8,1,1]{2,1,0:T(1,128)}), f32[8,1,1]{2,1,0:T(1,128)S(1)}, u32[]{:S(2)}, u32[]{:S(2)}) async-start(f32[8,1,1]{2,1,0:T(1,128)} %broadcast_in_dim.2), calls=%async_computation.4 | async-start | bytes 8192 | tf_op jit(solution)/shard_map/cond/branch_1_fun/all_to_all | solution.py:583
  490.2 55.7 %all-to-all-start.9 = ((f32[32,4,4096]{2,1,0:T(4,128)}), f32[32,4,4096]{2,1,0:T(4,128)S(1)}, u32[]{:S(2)}, u32[]{:S(2)}) async-start(f32[32,4,4096]{2,1,0:T(4,128)} %broadcast_in_dim.5), calls=%async_computation.9 | async-start | bytes 4194304 | tf_op jit(solution)/shard_map/cond/branch_1_fun/all_to_all | solution.py:583
  551.6 11.5 %all-to-all-start.10 = ((f32[8,1,4096]{2,1,0:T(1,128)}), f32[8,1,4096]{2,1,0:T(1,128)S(1)}, u32[]{:S(2)}, u32[]{:S(2)}) async-start(f32[8,1,4096]{2,1,0:T(1,128)} %broadcast_in_dim.6), calls=%async_computation.10 | async-start | bytes 262144 | tf_op jit(solution)/shard_map/cond/branch_1_fun/all_to_all | solution.py:583
  563.8 1.0 copy-start.7
  563.8 1.0 copy-start.8
